TPU v7x, 512 devices: a whole 4x4x16 slice. The times are simulated.
512 devices in a mesh: tx: 32 (over z, core), ty: 16 (over x, y).
Axes of the slice: x: 4, y: 4, z: 16, core: 2. Of those that a mesh axis runs over, the one named last changes fastest.
Arguments:
- object_planes: float32 [2, 8192, 8192], P(None, 'ty', 'tx'), may hold values from -6 to 6
- probe: float32 [2, 128, 128], replicated, may hold values from -6 to 6
- anchors: int32 [16, 32, 8, 2], P('ty', 'tx'), may hold values from 0 to 8064, as said below
- counts: int32 [16, 32], P('ty', 'tx'), may hold values from 1 to 7, as said below
- intensity: float32 [16, 32, 8, 128, 128], P('ty', 'tx'), may hold values from 0.1 to 3
Outputs:
- object_out: float32 [2, 8192, 8192], P(None, 'ty', 'tx')
- probe_out: float32 [2, 128, 128], replicated
Inputs may be any that keep to these rules, and one draw needn't show every extreme that they name: `counts`: each tile holds 1 to 7 live positions; tiles (a, b) and (a, b xor 32 / 2) together hold at most 8; in every draw some such pair holds exactly 8, one of them 8 - 1. `anchors`: every slot's corner lies inside its own tile, and its 128 x 128 patch lies inside the object.
All inputs are finite; a program needn't handle non-finite values.
Results may differ from a plain program's by a relative error of at most 0.0003.
Values sent between devices are 32-bit elements; how exact they have to be, the bound alone decides.
No kernel may reach another device: no remote copies, remote signals or barrier semaphores. Data moves between devices by JAX's collectives and lax.ppermute only.
A program may use at most 64 MiB of HBM per device.

v0:
```python
import jax
import jax.numpy as jnp
from jax import lax
from jax.sharding import PartitionSpec as P

ITERS = 2


step_object = 1.0
step_probe = 1.0


def from_behind(value, axis, steps):
    count = lax.axis_size(axis)
    leading, last = (max(0, -steps), min(count, count - steps))
    return lax.ppermute(value, axis, [(source, source + steps) for source in range(leading, last)])


def spectrum(field_re, field_im, table_re, table_im):
    best = lax.Precision.HIGHEST
    left_re = jnp.einsum("kn,snm->skm", table_re, field_re, precision=best) - jnp.einsum(
        "kn,snm->skm", table_im, field_im, precision=best
    )
    left_im = jnp.einsum("kn,snm->skm", table_re, field_im, precision=best) + jnp.einsum(
        "kn,snm->skm", table_im, field_re, precision=best
    )
    out_re = jnp.einsum("skm,mn->skn", left_re, table_re, precision=best) - jnp.einsum(
        "skm,mn->skn", left_im, table_im, precision=best
    )
    out_im = jnp.einsum("skm,mn->skn", left_re, table_im, precision=best) + jnp.einsum(
        "skm,mn->skn", left_im, table_re, precision=best
    )
    return (out_re, out_im)


def gradient_terms(patches, inten, weight, current, table_re, table_im):
    probe_re = current[0]
    probe_im = current[1]
    obj_re = patches[:, 0]
    obj_im = patches[:, 1]
    exit_re = probe_re * obj_re - probe_im * obj_im
    exit_im = probe_re * obj_im + probe_im * obj_re
    far_re, far_im = spectrum(exit_re, exit_im, table_re, table_im)
    misfit = far_re * far_re + far_im * far_im - inten
    back_re, back_im = spectrum(misfit * far_re, misfit * far_im, table_re, -table_im)
    back_re = back_re * weight[:, None, None]
    back_im = back_im * weight[:, None, None]
    obj_grad = jnp.stack(
        [probe_re * back_re + probe_im * back_im, probe_re * back_im - probe_im * back_re], axis=1
    )
    probe_grad = jnp.stack(
        [
            jnp.sum(obj_re * back_re + obj_im * back_im, axis=0),
            jnp.sum(obj_re * back_im - obj_im * back_re, axis=0),
        ]
    )
    return (obj_grad, probe_grad)


def body(object_planes, probe, anchors, counts, intensity):
    tile_rows = object_planes.shape[1]
    tile_cols = object_planes.shape[2]
    width = probe.shape[1]
    slots = anchors.shape[2]
    corner = jnp.stack([lax.axis_index("ty") * tile_rows, lax.axis_index("tx") * tile_cols])
    local = anchors[0, 0] - corner[None, :]
    count = counts[0, 0]
    inten = intensity[0, 0]
    slot_ids = jnp.arange(slots, dtype=jnp.int32)
    live = (slot_ids < count).astype(jnp.float32)
    freq = jnp.arange(width, dtype=jnp.int32)
    phase = (freq[:, None] * freq[None, :] % width).astype(jnp.float32) * (2.0 * jnp.pi / width)
    table_re = jnp.cos(phase) / jnp.sqrt(jnp.float32(width))
    table_im = -jnp.sin(phase) / jnp.sqrt(jnp.float32(width))
    planes = object_planes
    current = probe
    for step in range(ITERS):
        below = from_behind(planes[:, :width, :], "ty", -1)
        taller = jnp.concatenate([planes, below], axis=1)
        beside = from_behind(taller[:, :, :width], "tx", -1)
        extended = jnp.concatenate([taller, beside], axis=2)

        def cut_patch(spot):
            return lax.dynamic_slice(extended, (jnp.int32(0), spot[0], spot[1]), (2, width, width))

        patches = jax.vmap(cut_patch)(local)
        obj_grad, probe_grad = gradient_terms(patches, inten, live, current, table_re, table_im)

        def add_patch(index, total):
            spot = local[index]
            old = lax.dynamic_slice(total, (jnp.int32(0), spot[0], spot[1]), (2, width, width))
            return lax.dynamic_update_slice(
                total, old + obj_grad[index], (jnp.int32(0), spot[0], spot[1])
            )

        summed = lax.fori_loop(0, slots, add_patch, jnp.zeros_like(extended))
        col_rim = from_behind(summed[:, :, tile_cols:], "tx", 1)
        left_part = summed[:, :, :tile_cols].at[:, :, :width].add(col_rim)
        row_rim = from_behind(left_part[:, tile_rows:, :], "ty", 1)
        tile_grad = left_part[:, :tile_rows, :].at[:, :width, :].add(row_rim)
        total_probe = lax.psum(probe_grad, ("tx", "ty"))
        peak = jnp.max(current[0] * current[0] + current[1] * current[1]) + 1e-06
        planes = planes - step_object / peak * tile_grad
        current = current - step_probe / (lax.axis_size("tx") * lax.axis_size("ty")) * total_probe
    return (planes, current)


def solution(mesh):
    return jax.shard_map(
        body,
        mesh=mesh,
        in_specs=(
            P(None, "ty", "tx"),
            P(),
            P("ty", "tx", None, None),
            P("ty", "tx"),
            P("ty", "tx", None, None, None),
        ),
        out_specs=(P(None, "ty", "tx"), P()),
        check_vma=False,
    )
```

profile of v0, /device:TPU:1, one launch (start us, length us, event | category | flops | bytes accessed | tf_op | source)
XLA Modules:
  0.0 1188.6 jit_solution(3229713099765153430)
XLA Ops:
  11.7 4.3 collective-permute-done
  16.1 9.3 collective-permute-start.1
  25.4 6.0 collective-permute-done.1
  31.7 15.5 %while.34 = (s32[]{:T(128)}, f32[2,640,384]{2,1,0:T(8,128)S(1)}, s32[8,3]{0,1:T(4,128)S(1)}, f32[8,2,128,128]{3,2,0,1:T(8,128)S(1)}, s32[]{:T(128)}) while((s32[]{:T(128)}, f32[2,640,384]{2,1,0:T(8,128)S(1)}, s32[8,3]{0,1:T(4,128)S(1)}, f32[8,2,128,128]{3,2,0,1:T(8,128)S(1)}, s32[]{:T(128)}) %tuple.118), condition=%wide.while_cond.4, body=%wide.while_body.4.sunk | while | flops 2 | bytes 262261 | solution.py:84
  68.5 61.7 %while.32 = (s32[]{:T(128)}, f32[2,640,384]{2,1,0:T(8,128)S(1)}, s32[8,2]{0,1:T(2,128)S(1)}, f32[8,2,128,128]{3,2,0,1:T(8,128)}, s32[]{:T(128)}, /*index=5*/s32[]{:T(128)}, s32[]{:T(128)}, s32[]{:T(128)}) while((s32[]{:T(128)}, f32[2,640,384]{2,1,0:T(8,128)S(1)}, s32[8,2]{0,1:T(2,128)S(1)}, f32[8,2,128,128]{3,2,0,1:T(8,128)}, s32[]{:T(128)}, ...), condition=%wide.region_2.3_spmd, body=%wide.region_1.2_spmd.sunk | while | flops 32776 | bytes 655565 | solution.py:96
  81.5 2.5 dynamic_update_slice.16
  89.3 2.5 dynamic_update_slice.16
  97.0 2.5 dynamic_update_slice.16
  104.8 2.5 dynamic_update_slice.16
  127.7 2.5 dynamic_update_slice.16
  132.4 7.4 collective-permute-done.2
  141.0 3.5 collective-permute-start.3
  150.4 6.3 collective-permute-done.4
  159.4 462.1 %all-reduce.3.cloned.1.call-done = f32[2,128,128]{2,1,0:T(8,128)} async-done(((f32[2,128,128]{2,1,0:T(8,128)}), f32[2,128,128]{2,1,0:T(8,128)}) %all-reduce.3.cloned.1.call-update) | async-done | bytes 131088 | tf_op jit(solution)/shard_map/psum | solution.py:101
  622.4 2.5 pad_maximum_fusion.1
  625.0 23.9 %while.35 = (s32[]{:T(128)}, f32[2,640,384]{2,1,0:T(8,128)}, s32[8,3]{0,1:T(4,128)S(1)}, f32[8,2,128,128]{3,2,0,1:T(8,128)S(1)}, s32[]{:T(128)}) while((s32[]{:T(128)}, f32[2,640,384]{2,1,0:T(8,128)}, s32[8,3]{0,1:T(4,128)S(1)}, f32[8,2,128,128]{3,2,0,1:T(8,128)S(1)}, s32[]{:T(128)}) %tuple.134), condition=%wide.while_cond.5, body=%wide.while_body.5.sunk | while | flops 2 | bytes 262261 | solution.py:84
  669.4 63.8 %while.33 = (s32[]{:T(128)}, f32[2,640,384]{2,1,0:T(8,128)S(1)}, s32[8,2]{0,1:T(2,128)S(1)}, f32[8,2,128,128]{3,2,0,1:T(8,128)}, s32[]{:T(128)}, /*index=5*/s32[]{:T(128)}, s32[]{:T(128)}, s32[]{:T(128)}) while((s32[]{:T(128)}, f32[2,640,384]{2,1,0:T(8,128)S(1)}, s32[8,2]{0,1:T(2,128)S(1)}, f32[8,2,128,128]{3,2,0,1:T(8,128)}, s32[]{:T(128)}, ...), condition=%wide.region_8.9_spmd, body=%wide.region_7.8_spmd.sunk | while | flops 32776 | bytes 655565 | solution.py:96
  682.9 2.5 dynamic_update_slice.17
  690.9 2.5 dynamic_update_slice.17
  698.9 2.5 dynamic_update_slice.17
  706.9 2.5 dynamic_update_slice.17
  737.9 5.9 collective-permute-done.6
  746.8 2.7 collective-permute-start.7
  750.8 425.7 %all-reduce.5.cloned.1.call-done = f32[2,128,128]{2,1,0:T(8,128)} async-done(((f32[2,128,128]{2,1,0:T(8,128)}), f32[2,128,128]{2,1,0:T(8,128)}) %all-reduce.5.cloned.1.call-update) | async-done | bytes 131088 | tf_op jit(solution)/shard_map/psum | solution.py:101
  (206 shorter events, 153.2 us)
Async XLA Ops:
  7.2 4.4 copy-start.8
  7.2 614.3 %all-reduce.3.cloned.1.call-start = ((), (), s32[]{:S(2)}) async-start(), calls=%async_computation | async-start | bytes 262144 | tf_op jit(solution)/shard_map/psum | solution.py:101
  8.2 7.8 collective-permute-start
  9.5 15.9 %copy-start.3 = (f32[2,128,128]{2,1,0:T(8,128)S(1)}, f32[2,128,128]{2,1,0:T(8,128)}, u32[]{:S(2)}) copy-start(f32[2,128,128]{2,1,0:T(8,128)} %param.18) | copy-start | bytes 393220
  16.1 15.3 %collective-permute-start.1 = (f32[2,640,128]{2,1,0:T(8,128)S(1)}, f32[2,640,128]{2,1,0:T(8,128)S(1)}, u32[]{:S(2)}, u32[]{:S(2)}) collective-permute-start(f32[2,640,128]{2,1,0:T(8,128)S(1)} %slice.268), channel_id=1, source_target_pairs={{16,0},{32,16},{48,32},{64,48},{80,64},{96,80},{112,96},{128,112},... | collective-permute-start | bytes 1966088 | tf_op jit(solution)/shard_map/ppermute | solution.py:16
  54.2 2.3 copy-start
  130.3 14.2 %copy-start.4 = (f32[2,128,128]{2,1,0:T(8,128)S(1)}, f32[2,128,128]{2,1,0:T(8,128)}, u32[]{:S(2)}) copy-start(f32[2,128,128]{2,1,0:T(8,128)} %param.18) | copy-start | bytes 393220
  130.3 9.6 collective-permute-start.2
  139.9 1.1 copy-start.1
  141.0 7.8 copy-start.2
  141.0 6.7 collective-permute-start.3
  148.9 9.7 copy-start.6
  148.9 9.7 copy-start.7
  149.0 472.5 %copy-start.5 = (f32[2,128,128]{2,1,0:T(8,128)S(1)}, f32[2,128,128]{2,1,0:T(8,128)}, u32[]{:S(2)}) copy-start(f32[2,128,128]{2,1,0:T(8,128)} %param.18) | copy-start | bytes 393220
  149.0 7.7 collective-permute-start.4
  156.7 465.7 %collective-permute-start.5 = (f32[2,640,128]{2,1,0:T(8,128)S(1)}, f32[2,640,128]{2,1,0:T(8,128)}, u32[]{:S(2)}, u32[]{:S(2)}) collective-permute-start(f32[2,640,128]{2,1,0:T(8,128)S(1)} %pad_maximum_fusion.4), channel_id=1, source_target_pairs={{16,0},{32,16},{48,32},{64,48},{80,64},{96,80},{112,96},{128,112},... | collective-permute-start | bytes 1966088 | tf_op jit(solution)/shard_map/ppermute | solution.py:16
  159.4 1017.1 %all-reduce.5.cloned.1.call-start = ((), (), s32[]{:S(2)}) async-start(), calls=%async_computation.1 | async-start | bytes 262144 | tf_op jit(solution)/shard_map/psum | solution.py:101
  734.1 9.7 collective-permute-start.6
  746.8 432.6 %collective-permute-start.7 = (f32[2,128,256]{2,1,0:T(8,128)S(1)}, f32[2,128,256]{2,1,0:T(8,128)S(1)}, u32[]{:S(2)}, u32[]{:S(2)}) collective-permute-start(f32[2,128,256]{2,1,0:T(8,128)S(1)} %slice.277), channel_id=1, source_target_pairs={{0,1},{1,2},{2,3},{3,4},{4,5},{5,6},{6,7},{7,8},{8,9},{9,10},{10,1... | collective-permute-start | bytes 786440 | tf_op jit(solution)/shard_map/ppermute | solution.py:16
Sparse Core Ops, SparseCore 0:
  159.5 461.9 all-reduce.2
  738.0 438.4 all-reduce.4
where the time goes:
time: 1200 us; the launch traced here: 1190 us
  waiting for transfers between devices  918 us (76%)
  local copies, waits for them, and re-layouts  97.8 us (8%)
  loops' own time  60.4 us (5%)
  matrix products  39.3 us (3%)
  other arithmetic  31.6 us (3%)
  starting transfers between devices  24.1 us (2%)
  between operations  16.9 us (1%)
    psum x2, waiting for transfers between devices, body(): total_probe = lax.psum(probe_grad, ('tx', 'ty'))  888 us
    another operation x2, loops' own time, body(): summed = lax.fori_loop(0, slots, add_patch, jnp.zeros_like(extended))  59.9 us
    dynamic_update_slice x16, local copies, waits for them, and re-layouts, add_patch(): lax.dynamic_update_slice(total, old + obj_grad[index], (jnp.int32(0), spo...  39.3 us
    gather x48, local copies, waits for them, and re-layouts  38.8 us
    ppermute x8, waiting for transfers between devices, from_behind(): lax.ppermute(value, axis, [(source, source + steps) for source in range(l...  30.6 us
    ppermute x8, starting transfers between devices, from_behind(): lax.ppermute(value, axis, [(source, source + steps) for source in range(l...  24 us
  transfers between devices with their start and end apart: 10, of which 8 were waited for; matrix products, arithmetic and copies ran while one was open for 1% of the time, Pallas kernels for 0%

commit v1 on v0

v1 whole, which is shorter than its diff:
```python
import jax
import jax.numpy as jnp
import numpy as np
from jax import lax
from jax.experimental import pallas as pl
from jax.experimental.pallas import tpu as pltpu
from jax.sharding import PartitionSpec as P

step_object = 1.0
step_probe = 1.0
GROUP = 2
CORES = 2
F32 = jnp.float32
BF16 = jnp.bfloat16


def shift(value, rows, cols):
    n_r, n_c = lax.axis_size("ty"), lax.axis_size("tx")
    if cols == 0:
        return lax.ppermute(
            value, "ty", [(a, a + rows) for a in range(n_r) if 0 <= a + rows < n_r]
        )
    if rows == 0:
        return lax.ppermute(
            value, "tx", [(b, b + cols) for b in range(n_c) if 0 <= b + cols < n_c]
        )
    pairs = [
        (b * n_r + a, (b + cols) * n_r + a + rows)
        for a in range(n_r)
        for b in range(n_c)
        if 0 <= a + rows < n_r and 0 <= b + cols < n_c
    ]
    return lax.ppermute(value, ("tx", "ty"), pairs)


def swap(parts, axes, groups):
    return lax.all_to_all(parts, axes, 0, 0, axis_index_groups=groups, tiled=True)


def device_groups():
    n_r, n_c = lax.axis_size("ty"), lax.axis_size("tx")
    depth = n_c // CORES
    plane = [
        [(z * CORES + c) * n_r + a for c in range(CORES) for a in range(n_r)] for z in range(depth)
    ]
    near = min(4, depth)

    def along(step, size):
        return [
            [(first + i * step) * CORES + c for i in range(size)]
            for c in range(CORES)
            for first in range(depth)
            if first // step % size == 0
        ]

    return plane, along(1, near), along(near, depth // near)


def sum_in_plane(value):
    plane, near, far = device_groups()
    parts = value.reshape(len(plane[0]), -1, value.shape[-1])
    return fold(swap(parts, ("tx", "ty"), plane), len(near[0]), "fold_plane")


def sum_along(parts):
    plane, near, far = device_groups()
    parts = fold(swap(parts, "tx", near), len(far[0]), "fold_near")
    parts = fold(swap(parts, "tx", far), len(plane[0]), "fold_far")
    parts = swap(parts, ("tx", "ty"), plane)
    return parts.reshape(2, -1, parts.shape[-1])


def fold(parts, copies, name):
    (out,) = call(fold_kernel, name, (), (), [(copies, *parts.shape[1:])], [], 1, 1)(parts)
    return out


def fold_kernel(parts, out, sems):
    mine = parts[0]
    for at in range(1, parts.shape[0]):
        mine += parts[at]
    for at in range(out.shape[0]):
        out[at] = mine


def dft_table(width):
    index = np.arange(width)
    angle = 2.0 * np.pi * ((index[:, None] * index[None, :]) % width) / width
    cos, sin = np.cos(angle) / np.sqrt(width), -np.sin(angle) / np.sqrt(width)
    table = np.block([[cos, sin], [-sin, cos]]).astype(np.float32)
    lead = table.astype(jnp.bfloat16)
    trail = (table - lead.astype(np.float32)).astype(jnp.bfloat16)
    return np.concatenate([lead, lead, trail], axis=0)


def transform(re, im, table):
    rows = jnp.concatenate([re, im], axis=1)
    lead = rows.astype(BF16)
    trail = (rows - lead.astype(F32)).astype(BF16)
    out = jnp.dot(
        jnp.concatenate([lead, trail, lead], axis=1), table[...], preferred_element_type=F32
    )
    width = re.shape[1]
    return out[:, :width], out[:, width:]


def turn(parts):
    return jnp.concatenate([jnp.transpose(part) for part in parts], axis=0)


def add_slots(org, count, ext, acc, probe_re, probe_im, total, inten, table):
    width = probe_re.shape[0]
    bottom = ext.shape[2] - width
    lanes = lax.broadcasted_iota(jnp.int32, (width, width), 1)

    def split(value):
        return [value[i * width : (i + 1) * width] for i in range(GROUP)]

    def some(step, carry):
        slots = [step * GROUP + i for i in range(GROUP)]
        rows, blocks, cols, masks = [], [], [], []
        weights = []
        for slot in slots:
            col = lax.rem(org[1, slot], (ext.shape[1] - 1) * width)
            rows.append(lax.rem(org[0, slot], bottom))
            blocks.append(col // width)
            cols.append(lax.rem(col, width))
            masks.append(lanes >= cols[-1])
            weights.append((slot < count).astype(F32))
        obj, prb = [], []
        for i in range(GROUP):
            where = pl.ds(rows[i], width)
            obj.append(
                [
                    jnp.where(masks[i], ext[p, blocks[i], where, :], ext[p, blocks[i] + 1, where, :])
                    for p in range(2)
                ]
            )
            prb.append([pltpu.roll(part, cols[i], 1) for part in (probe_re, probe_im)])
        wave_re = [p[0] * o[0] - p[1] * o[1] for p, o in zip(prb, obj)]
        wave_im = [p[0] * o[1] + p[1] * o[0] for p, o in zip(prb, obj)]
        half_re, half_im = transform(
            jnp.concatenate(wave_re, axis=0), jnp.concatenate(wave_im, axis=0), table
        )
        far_re, far_im = transform(turn(split(half_re)), turn(split(half_im)), table)
        seen = jnp.concatenate([inten[slot] for slot in slots], axis=0)
        misfit = far_re * far_re + far_im * far_im - seen
        misfit = jnp.concatenate([m * w for m, w in zip(split(misfit), weights)], axis=0)
        half_im, half_re = transform(misfit * far_im, misfit * far_re, table)
        back_im, back_re = transform(turn(split(half_im)), turn(split(half_re)), table)
        back_re, back_im = split(back_re), split(back_im)
        sums = [jnp.zeros((width, width), F32)] * 2
        for i in range(GROUP):
            where = pl.ds(rows[i], width)
            grad = (
                prb[i][0] * back_re[i] + prb[i][1] * back_im[i],
                prb[i][0] * back_im[i] - prb[i][1] * back_re[i],
            )
            for p in range(2):
                acc[p, blocks[i], where, :] += jnp.where(masks[i], grad[p], 0.0)
                acc[p, blocks[i] + 1, where, :] += jnp.where(masks[i], 0.0, grad[p])
            own = (
                obj[i][0] * back_re[i] + obj[i][1] * back_im[i],
                obj[i][0] * back_im[i] - obj[i][1] * back_re[i],
            )
            home = lax.rem(width - cols[i], width)
            sums = [s + pltpu.roll(o, home, 1) for s, o in zip(sums, own)]
        for p in range(2):
            total[p] += sums[p]
        return carry

    lax.fori_loop(0, (count + GROUP - 1) // GROUP, some, 0)


def peak_of(probe_re, probe_im):
    power = probe_re * probe_re + probe_im * probe_im
    top = jnp.max(jnp.max(power, axis=0, keepdims=True), axis=1, keepdims=True)
    return step_object / (top + 1e-6)


class Copies:
    def __init__(self, sems):
        self.sems, self.used = sems, 0

    def start(self, *pairs):
        out = []
        for source, target in pairs:
            out.append(pltpu.make_async_copy(source, target, self.sems.at[self.used]))
            out[-1].start()
            self.used += 1
        return out


def wait(copies):
    for copy in copies:
        copy.wait()


def pack_kernel(tile, below, right, corner, sems):
    width = right.shape[2]
    wait(
        Copies(sems).start(
            (tile.at[:, :width, :], below),
            (tile.at[:, :, :width], right),
            (tile.at[:, :width, :width], corner),
        )
    )


def prepare_kernel(
    tile, probe_in, inten_in, table_in, ext, probe, inten, table, inten_out, raw, sems
):
    width = ext.shape[3]
    bottom = tile.shape[1]
    copies = Copies(sems)
    first = copies.start((inten_in, raw))
    rest = copies.start((probe_in, probe), (table_in, table))
    for j in range(ext.shape[1] - 1):
        rest += copies.start((tile.at[:, :, pl.ds(j * width, width)], ext.at[:, j, :bottom]))
    wait(first)
    for slot in range(raw.shape[0]):
        inten[slot] = jnp.transpose(raw[slot])
    wait(rest + copies.start((inten, inten_out)))


def first_kernel(
    org, counts, ext_in, below, right, corner, probe, inten, table,
    ext, acc_0, acc_1, acc_2, up, down, total, acc, sems,
):
    n = ext.shape[1] - 1
    width = ext.shape[3]
    bottom = ext.shape[2] - width
    for p in range(2):
        for j in range(n):
            ext[p, j, bottom:] = below[p, :, j * width : (j + 1) * width]
        ext[p, n, :bottom] = right[p]
        ext[p, n, bottom:] = corner[p]
    acc[...] = jnp.zeros_like(acc)
    total[...] = jnp.zeros_like(total)
    add_slots(org, counts[0], ext, acc, probe[0], probe[1], total, inten, table)
    for p in range(2):
        for j, part in enumerate((acc_0, acc_1, acc_2)):
            part[p] = acc[p, j]
            up[p, j] = acc[p, j, :width]
            down[p, j] = acc[p, j, bottom:]


def corners_kernel(from_up, from_down, after, to_left, to_right, sems):
    del after
    last = from_up.shape[1] - 1
    for p in range(2):
        for at, block in enumerate((from_up, from_down)):
            to_left[p, at] = block[p, 0]
            to_right[p, at] = block[p, last]


def second_kernel(
    org, counts, ext, acc_0, acc_1, acc_2, from_left, from_right, from_up, from_down,
    more_left, more_right, probe_in, gathered, share, inten_in, table_in,
    obj_out, side_out, probe_out, total_out, right_out, down_out, corner_out,
    cur, acc, own, probe, total, inten, table, sems,
):
    n = cur.shape[1] - 1
    width = cur.shape[3]
    bottom = cur.shape[2] - width
    copies = Copies(sems)
    loads = copies.start((inten_in, inten), (table_in, table))
    scale = peak_of(probe_in[0], probe_in[1])
    mid = slice(width, bottom)
    for p in range(2):
        probe[p] = probe_in[p] - share[0] * gathered[p]
        rows = ((slice(0, width), from_up, 0), (mid, None, 0), (slice(bottom, None), from_down, 1))
        for j, (part, side, more) in enumerate(
            ((acc_0, from_left, more_left), (acc_1, None, None), (acc_2, from_right, more_right))
        ):
            for where, edge, at in rows:
                value = part[p, where]
                if side is not None:
                    value += side[p, where]
                if edge is not None:
                    value += edge[p, j]
                    if more is not None:
                        value += more[p, at]
                cur[p, j, where] = ext[p, j, where] - scale * value
    acc[...] = jnp.zeros_like(acc)
    total[...] = jnp.zeros_like(total)
    wait(loads)
    add_slots(org, counts[0], cur, acc, probe[0], probe[1], total, inten, table)
    stores = copies.start((total, total_out), (probe, probe_out))
    scale = peak_of(probe[0], probe[1])
    for p in range(2):
        for j in range(n):
            own[p, j] = cur[p, j, :bottom] - scale * acc[p, j, :bottom]
            acc[p, j, bottom:] = scale * acc[p, j, bottom:]
        acc[p, n] = scale * acc[p, n]
    stores += copies.start(
        (acc.at[:, n, :bottom], right_out), (acc.at[:, n, bottom:], corner_out),
        (acc.at[:, :n, bottom:], down_out), (own.at[:, 0], side_out),
    )
    for j in range(1, n):
        cols = pl.ds(j * width, width)
        stores += copies.start((own.at[:, j], obj_out.at[:, :, cols]))
    wait(stores)


def final_kernel(
    obj_in, side_in, probe_in, from_left, from_up, from_corner, gathered, share,
    obj_out, probe_out, side, top, probe, sems,
):
    width = side.shape[2]
    copies = Copies(sems)
    places = [pl.ds((j + 1) * width, width) for j in range(top.shape[1])]
    loads = copies.start((side_in, side), (probe_in, probe))
    for j, cols in enumerate(places):
        loads += copies.start((obj_in.at[:, :width, cols], top.at[:, j]))
    wait(loads)
    for p in range(2):
        side[p] -= from_left[p]
        side[p, :width] -= from_up[p, 0] + from_corner[p]
        for j in range(top.shape[1]):
            top[p, j] -= from_up[p, j + 1]
        probe[p] -= share[0] * gathered[p]
    stores = copies.start((side, obj_out.at[:, :, :width]), (probe, probe_out))
    for j, cols in enumerate(places):
        stores += copies.start((top.at[:, j], obj_out.at[:, :width, cols]))
    wait(stores)


def call(kernel, name, smem, far, outs, scratch, copies, mib, **more):
    kinds = {True: pltpu.HBM, False: pltpu.VMEM}

    def run(*operands):
        where = [pltpu.SMEM if at in smem else kinds[at in far] for at in range(len(operands))]
        held = [kinds[-1 - at in far] for at in range(len(outs))]
        operands = [
            value if space is pltpu.SMEM else pltpu.with_memory_space_constraint(value, space)
            for value, space in zip(operands, where)
        ]
        return pl.pallas_call(
            kernel,
            out_shape=[space(s, F32) if isinstance(s, tuple) else space(s.shape, s.dtype) for s, space in zip(outs, held)],
            in_specs=[pl.BlockSpec(memory_space=space) for space in where],
            out_specs=[pl.BlockSpec(memory_space=space) for space in held],
            scratch_shapes=[
                *(pltpu.VMEM(s, F32) if isinstance(s, tuple) else pltpu.VMEM(s.shape, s.dtype) for s in scratch),
                pltpu.SemaphoreType.DMA((copies,)),
            ],
            compiler_params=pltpu.CompilerParams(vmem_limit_bytes=mib * 1024 * 1024),
            name=name,
            **more,
        )(*operands)

    return run


def body(object_planes, probe, anchors, counts, intensity):
    rows, cols = object_planes.shape[1:]
    w = probe.shape[1]
    org = anchors[0, 0].T
    count = counts[0]
    inten = intensity[0, 0]
    table = jnp.asarray(dft_table(w))
    kept = jax.ShapeDtypeStruct(table.shape, table.dtype)
    slots = inten.shape
    n = cols // w
    tall, square = (2, rows + w, w), (2, w, w)
    blocks, strip = (2, n + 1, rows + w, w), (2, n + 1, w, w)
    share = jnp.full((1,), step_probe / (lax.axis_size("tx") * lax.axis_size("ty")), F32)

    below, right, corner = call(
        pack_kernel, "pack", (), (0,), [(2, w, cols), (2, rows, w), square], [], 3, 2
    )(object_planes)
    right, below, corner = shift(right, 0, -1), shift(below, -1, 0), shift(corner, -1, -1)
    ext, start, inten_near, table_near, inten = call(
        prepare_kernel, "prepare", (), (0, 1, 2, 3, -5),
        [blocks, square, slots, kept, slots], [slots], 6, 4,
    )(object_planes, probe, inten, table)
    ext, acc_0, acc_1, acc_2, up, down, total = call(
        first_kernel, "first_pass", (0, 1), (), [blocks, tall, tall, tall, strip, strip, square],
        [blocks], 1, 6, input_output_aliases={2: 0},
    )(org, count, ext, below, right, corner, start, inten_near, table_near)
    from_left, from_right = shift(acc_2, 0, 1), shift(acc_0, 0, -1)
    from_up, from_down = shift(down, 1, 0), shift(up, -1, 0)
    parts = sum_in_plane(total)
    to_left, to_right = call(
        corners_kernel, "corners", (), (), [(2, 2, w, w)] * 2, [], 1, 1
    )(from_up, from_down, parts)
    more_left, more_right = shift(to_right, 0, 1), shift(to_left, 0, -1)
    gathered = sum_along(parts)
    obj, side, current, total, to_right, to_down, to_corner = call(
        second_kernel, "second_pass", (0, 1, 14), (15, 16, *range(-7, 0)),
        [(2, rows, cols), (2, rows, w), square, square, (2, rows, w), (2, n, w, w), square],
        [blocks, blocks, (2, n, rows, w), square, square, slots, kept], n + 7, 9,
    )(
        org, count, ext, acc_0, acc_1, acc_2, from_left, from_right, from_up, from_down,
        more_left, more_right, start, gathered, share, inten, table,
    )
    from_left, from_up = shift(to_right, 0, 1), shift(to_down, 1, 0)
    from_corner = shift(to_corner, 1, 1)
    gathered = sum_along(sum_in_plane(total))
    obj, current = call(
        final_kernel, "finish", (7,), (0, 1, 2, -1, -2), [(2, rows, cols), square],
        [(2, rows, w), (2, n - 1, w, w), square], 2 * n + 2, 3, input_output_aliases={0: 0},
    )(obj, side, current, from_left, from_up, from_corner, gathered, share)
    return obj, current


def solution(mesh):
    return jax.shard_map(
        body,
        mesh=mesh,
        in_specs=(
            P(None, "ty", "tx"),
            P(),
            P("ty", "tx", None, None),
            P("ty", "tx"),
            P("ty", "tx", None, None, None),
        ),
        out_specs=(P(None, "ty", "tx"), P()),
        check_vma=False,
    )
```

time: 1200 us -> 170 us (0.14)
  waiting for transfers between devices: 918 us -> 25 us
  local copies, waits for them, and re-layouts: 97.8 us -> 0.01 us
  blocking collectives: 0 us -> 68.2 us
  loops' own time: 60.4 us -> 0 us
  matrix products: 39.3 us -> 0 us
  starting transfers between devices: 24.1 us -> 57.4 us
  other arithmetic: 31.6 us -> 0 us
  Pallas kernels: 0 us -> 16.9 us
  between operations: 16.9 us -> 1.53 us
    psum x2 -> x0, waiting for transfers between devices: 888 us -> none  [body(): total_probe = lax.psum(probe_grad, ('tx', 'ty'))]
    all_to_all x0 -> x5, blocking collectives: none -> 68.2 us  [swap(): lax.all_to_all(parts, axes, 0, 0, axis_index_groups=groups, tiled=True)]
    another operation x4 -> x0, loops' own time: 60.4 us -> none  [the longest x2 59.9 us: body(): summed = lax.fori_loop(0, slots, add_patch, jnp.zeros_like(extended))]
    dynamic_update_slice x16 -> x0, local copies, waits for them, and re-layouts: 39.3 us -> none  [add_patch(): lax.dynamic_update_slice(total, old + obj_grad[index], (jnp.int32(0), spo...]
    dot_general x32 -> x0, matrix products: 39.3 us -> none  [the longest x4 5.64 us: spectrum(): jnp.einsum('skm,mn->skn', left_im, table_im, precision=best)]
    gather x48 -> x0, local copies, waits for them, and re-layouts: 38.8 us -> none
    ppermute x8 -> x12, waiting for transfers between devices: 30.6 us -> 5.98 us  [the longest x2 3.24 us: shift(): return lax.ppermute(value, ('tx', 'ty'), pairs)]
    all_to_all x0 -> x3, waiting for transfers between devices: none -> 19 us  [swap(): lax.all_to_all(parts, axes, 0, 0, axis_index_groups=groups, tiled=True)]
  transfers between devices with their start and end apart: 10 -> 15, of which waited for: 8 -> 5; matrix products, arithmetic and copies ran while one was open for 1% -> 0% of each run, Pallas kernels for 0% -> 2%
where the time goes in v1:
time: 170 us; the launch traced here: 169 us
  blocking collectives  68.2 us (40%)
  starting transfers between devices  57.4 us (34%)
  waiting for transfers between devices  25 us (15%)
  Pallas kernels  16.9 us (10%)
    all_to_all x5, blocking collectives, swap(): lax.all_to_all(parts, axes, 0, 0, axis_index_groups=groups, tiled=True)  68.2 us
    ppermute x6, starting transfers between devices, shift(): lax.ppermute(value, 'tx', [(b, b + cols) for b in range(n_c) if 0 <= b +...  25.2 us
    all_to_all x3, waiting for transfers between devices, swap(): lax.all_to_all(parts, axes, 0, 0, axis_index_groups=groups, tiled=True)  19 us
    pallas_call x12, Pallas kernels, run(): pl.pallas_call(kernel, out_shape=[space(s, F32) if isinstance(s, tuple) e...  16.9 us
    all_to_all x3, starting transfers between devices, swap(): lax.all_to_all(parts, axes, 0, 0, axis_index_groups=groups, tiled=True)  16.6 us
    ppermute x4, starting transfers between devices, shift(): lax.ppermute(value, 'ty', [(a, a + rows) for a in range(n_r) if 0 <= a +...  10.1 us
    ppermute x2, starting transfers between devices, shift(): return lax.ppermute(value, ('tx', 'ty'), pairs)  5.56 us
  transfers between devices with their start and end apart: 15, of which 5 were waited for; matrix products, arithmetic and copies ran while one was open for 0% of the time, Pallas kernels for 2%

profile of v1, /device:TPU:1, one launch (start us, length us, event | category | flops | bytes accessed | tf_op | source)
XLA Modules:
  0.0 169.0 jit_solution(1865389455075040975)
XLA Ops:
  1.8 8.8 %collective-permute-start.1 = (f32[2,512,128]{2,1,0:T(8,128)S(1)}, f32[2,512,128]{2,1,0:T(8,128)S(1)}, u32[]{:S(2)}, u32[]{:S(2)}) collective-permute-start(f32[2,512,128]{2,1,0:T(8,128)S(1)} %get-tuple-element.28), channel_id=1, source_target_pairs={{16,0},{32,16},{48,32},{64,48},{80,64},{96,80},{112,96},{128,112},... | collective-permute-start | bytes 1572872 | tf_op jit(solution)/shard_map/ppermute | solution.py:24
  13.9 2.1 %prepare.1 = (f32[2,3,640,128]{3,2,1,0:T(8,128)S(1)}, f32[2,128,128]{2,1,0:T(8,128)S(1)}, f32[8,128,128]{2,1,0:T(8,128)S(1)}, bf16[768,256]{1,0:T(8,128)(2,1)S(1)}, f32[8,128,128]{2,1,0:T(8,128)}) custom-call(f32[2,512,256]{2,1,0:T(8,128)} %tile.3, f32[2,128,128]{2,1,0:T(8,128)} %probe_in.1, f32[8,128,128]{2,1,0:T(8,128)} %bitcast.16, ...), custom_call_target="tpu_custom_call" | custom-call | tf_op jit(solution)/shard_map/prepare/pallas_call | solution.py:339
  16.0 3.2 %collective-permute-done.2.corner = f32[2,128,128]{2,1,0:T(8,128)S(1)} collective-permute-done((f32[2,128,128]{2,1,0:T(8,128)S(1)}, f32[2,128,128]{2,1,0:T(8,128)S(1)}, u32[]{:S(2)}, u32[]{:S(2)}) %collective-permute-start.2) | collective-permute-done | bytes 131104 | tf_op jit(solution)/shard_map/ppermute | solution.py:33
  19.2 2.7 %collective-permute-done.below = f32[2,128,256]{2,1,0:T(8,128)S(1)} collective-permute-done((f32[2,128,256]{2,1,0:T(8,128)S(1)}, f32[2,128,256]{2,1,0:T(8,128)S(1)}, u32[]{:S(2)}, u32[]{:S(2)}) %collective-permute-start) | collective-permute-done | bytes 262176 | tf_op jit(solution)/shard_map/ppermute | solution.py:20
  21.9 3.8 %first_pass.1 = (f32[2,3,640,128]{3,2,1,0:T(8,128)S(1)}, f32[2,640,128]{2,1,0:T(8,128)S(1)}, f32[2,640,128]{2,1,0:T(8,128)S(1)}, f32[2,640,128]{2,1,0:T(8,128)S(...) custom-call(s32[2,8]{1,0:T(2,128)S(1)} %bitcast.14, ...), custom_call_target="tpu_custom_call", output_to_operand_aliasing={{0}: (2, {})} | custom-call | tf_op jit(solution)/shard_map/first_pass/pallas_call | solution.py:339
  25.7 4.2 %collective-permute-start.5 = (f32[2,3,128,128]{3,2,1,0:T(8,128)S(1)}, f32[2,3,128,128]{3,2,1,0:T(8,128)S(1)}, u32[]{:S(2)}, u32[]{:S(2)}) collective-permute-start(f32[2,3,128,128]{3,2,1,0:T(8,128)S(1)} %get-tuple-element.37), channel_id=1, source_target_pairs={{0,1},{1,2},{2,3},{3,4},{4,5},{5,6},{6,7},{7,8},{8,9},{9,10},{10,1... | collective-permute-start | bytes 1179656 | tf_op jit(solution)/shard_map/ppermute | solution.py:20
  33.2 3.6 %collective-permute-start.3 = (f32[2,640,128]{2,1,0:T(8,128)S(1)}, f32[2,640,128]{2,1,0:T(8,128)S(1)}, u32[]{:S(2)}, u32[]{:S(2)}) collective-permute-start(f32[2,640,128]{2,1,0:T(8,128)S(1)} %get-tuple-element.36.acc_2), channel_id=1, source_target_pairs={{0,16},{16,32},{32,48},{48,64},{64,80},{80,96},{96,112},{112,128},... | collective-permute-start | bytes 1966088 | tf_op jit(solution)/shard_map/ppermute | solution.py:24
  36.8 12.1 %all_to_all.40.parts = f32[32,8,128]{2,1,0:T(8,128)S(1)} all-to-all(f32[32,8,128]{2,1,0:T(8,128)S(1)} %bitcast.13), channel_id=1, replica_groups={{0,1,2,3,4,5,6,7,8,9,10,11,12,13,14,15,16,17,18,19,20,21,22,23,24,25,26..., dimensions={0} | all-to-all | bytes 262144 | tf_op jit(solution)/shard_map/all_to_all | solution.py:37
  49.0 6.0 %collective-permute-start.7 = (f32[2,2,128,128]{3,2,1,0:T(8,128)S(1)}, f32[2,2,128,128]{3,2,1,0:T(8,128)S(1)}, u32[]{:S(2)}, u32[]{:S(2)}) collective-permute-start(f32[2,2,128,128]{3,2,1,0:T(8,128)S(1)} %get-tuple-element.40), channel_id=1, source_target_pairs={{0,16},{16,32},{32,48},{48,64},{64,80},{80,96},{96,112},{112,128},... | collective-permute-start | bytes 786440 | tf_op jit(solution)/shard_map/ppermute | solution.py:24
  56.9 12.1 %all_to_all.41.parts = f32[4,8,128]{2,1,0:T(8,128)S(1)} all-to-all(f32[4,8,128]{2,1,0:T(8,128)S(1)} %fold_plane.2.after), channel_id=1, replica_groups={{0,32,64,96},{128,160,192,224},{256,288,320,352},{384,416,448,480},{16,..., dimensions={0} | all-to-all | bytes 32768 | tf_op jit(solution)/shard_map/all_to_all | solution.py:37
  69.1 20.9 %all_to_all.42.parts = f32[4,8,128]{2,1,0:T(8,128)S(1)} all-to-all(f32[4,8,128]{2,1,0:T(8,128)S(1)} %fold_near.2), channel_id=1, replica_groups={{0,128,256,384},{32,160,288,416},{64,192,320,448},{96,224,352,480},{16,..., dimensions={0} | all-to-all | bytes 32768 | tf_op jit(solution)/shard_map/all_to_all | solution.py:37
  90.0 15.8 %all_to_all.43 = f32[32,8,128]{2,1,0:T(8,128)S(1)} all-to-all(f32[32,8,128]{2,1,0:T(8,128)S(1)} %fold_far.2), channel_id=1, replica_groups={{0,1,2,3,4,5,6,7,8,9,10,11,12,13,14,15,16,17,18,19,20,21,22,23,24,25,26..., dimensions={0} | all-to-all | bytes 262144 | tf_op jit(solution)/shard_map/all_to_all | solution.py:37
  105.8 6.2 %second_pass.1 = (f32[2,512,256]{2,1,0:T(8,128)}, f32[2,512,128]{2,1,0:T(8,128)}, f32[2,128,128]{2,1,0:T(8,128)}, f32[2,128,128]{2,1,0:T(8,128)}, f32[2,512,128]...) custom-call(s32[2,8]{1,0:T(2,128)S(1)} %bitcast.15, s32[1]{0:T(128)} %bitcast.10.counts, ...), custom_call_target="tpu_custom_call" | custom-call | tf_op jit(solution)/shard_map/second_pass/pallas_call | solution.py:339
  112.1 2.9 %collective-permute-start.9 = (f32[2,512,128]{2,1,0:T(8,128)}, f32[2,512,128]{2,1,0:T(8,128)S(1)}, u32[]{:S(2)}, u32[]{:S(2)}) collective-permute-start(f32[2,512,128]{2,1,0:T(8,128)} %get-tuple-element.46), channel_id=1, source_target_pairs={{0,16},{16,32},{32,48},{48,64},{64,80},{80,96},{96,112},{112,128},... | collective-permute-start | bytes 1572872 | tf_op jit(solution)/shard_map/ppermute | solution.py:24
  115.0 4.5 %all-to-all-start.4 = ((f32[32,8,128]{2,1,0:T(8,128)}), f32[32,8,128]{2,1,0:T(8,128)S(1)}, u32[]{:S(2)}, u32[]{:S(2)}) async-start(f32[32,8,128]{2,1,0:T(8,128)} %bitcast.17), calls=%async_computation.4 | async-start | bytes 262144 | tf_op jit(solution)/shard_map/all_to_all | solution.py:37
  119.5 3.3 %collective-permute-start.10 = (f32[2,2,128,128]{3,2,1,0:T(8,128)}, f32[2,2,128,128]{3,2,1,0:T(8,128)S(1)}, u32[]{:S(2)}, u32[]{:S(2)}) collective-permute-start(f32[2,2,128,128]{3,2,1,0:T(8,128)} %get-tuple-element.47), channel_id=1, source_target_pairs={{0,1},{1,2},{2,3},{3,4},{4,5},{5,6},{6,7},{7,8},{8,9},{9,10},{10,1... | collective-permute-start | bytes 786440 | tf_op jit(solution)/shard_map/ppermute | solution.py:20
  122.8 4.2 %all-to-all-done.4.parts = f32[32,8,128]{2,1,0:T(8,128)S(1)} async-done(((f32[32,8,128]{2,1,0:T(8,128)}), f32[32,8,128]{2,1,0:T(8,128)S(1)}, u32[]{:S(2)}, u32[]{:S(2)}) %all-to-all-start.4) | async-done | bytes 131104 | tf_op jit(solution)/shard_map/all_to_all | solution.py:37
  127.1 7.3 %all_to_all.44.parts = f32[4,8,128]{2,1,0:T(8,128)S(1)} all-to-all(f32[4,8,128]{2,1,0:T(8,128)S(1)} %fold_plane.3), channel_id=1, replica_groups={{0,32,64,96},{128,160,192,224},{256,288,320,352},{384,416,448,480},{16,..., dimensions={0} | all-to-all | bytes 32768 | tf_op jit(solution)/shard_map/all_to_all | solution.py:37
  135.0 5.0 %all-to-all-start.6 = ((f32[4,8,128]{2,1,0:T(8,128)}), f32[4,8,128]{2,1,0:T(8,128)S(1)}, u32[]{:S(2)}, u32[]{:S(2)}) async-start(f32[4,8,128]{2,1,0:T(8,128)} %fold_near.3), calls=%async_computation.6 | async-start | bytes 32768 | tf_op jit(solution)/shard_map/all_to_all | solution.py:37
  140.1 4.3 %collective-permute-start.11 = (f32[2,128,128]{2,1,0:T(8,128)}, f32[2,128,128]{2,1,0:T(8,128)S(1)}, u32[]{:S(2)}, u32[]{:S(2)}) collective-permute-start(f32[2,128,128]{2,1,0:T(8,128)} %get-tuple-element.48), channel_id=1, source_target_pairs={{0,17},{16,33},{32,49},{48,65},{64,81},{80,97},{96,113},{112,129},... | collective-permute-start | bytes 393224 | tf_op jit(solution)/shard_map/ppermute | solution.py:33
  144.4 7.3 %all-to-all-done.6.parts = f32[4,8,128]{2,1,0:T(8,128)S(1)} async-done(((f32[4,8,128]{2,1,0:T(8,128)}), f32[4,8,128]{2,1,0:T(8,128)S(1)}, u32[]{:S(2)}, u32[]{:S(2)}) %all-to-all-start.6) | async-done | bytes 16416 | tf_op jit(solution)/shard_map/all_to_all | solution.py:37
  152.3 7.1 %all-to-all-start.7 = ((f32[32,8,128]{2,1,0:T(8,128)}), f32[32,8,128]{2,1,0:T(8,128)S(1)}, u32[]{:S(2)}, u32[]{:S(2)}) async-start(f32[32,8,128]{2,1,0:T(8,128)} %fold_far.3), calls=%async_computation.7 | async-start | bytes 262144 | tf_op jit(solution)/shard_map/all_to_all | solution.py:37
  159.4 7.5 %all-to-all-done.7 = f32[32,8,128]{2,1,0:T(8,128)S(1)} async-done(((f32[32,8,128]{2,1,0:T(8,128)}), f32[32,8,128]{2,1,0:T(8,128)S(1)}, u32[]{:S(2)}, u32[]{:S(2)}) %all-to-all-start.7) | async-done | bytes 131104 | tf_op jit(solution)/shard_map/all_to_all | solution.py:37
  166.9 2.1 %finish.1 = (f32[2,512,256]{2,1,0:T(8,128)}, f32[2,128,128]{2,1,0:T(8,128)}) custom-call(f32[2,512,256]{2,1,0:T(8,128)} %get-tuple-element.43.obj_in, f32[2,512,128]{2,1,0:T(8,128)} %get-tuple-element.44.side_in, f32[2,128,128]{2,1,0:T(8,128)} %get-tuple-element.45.probe_in, ...), custom_call_target="tpu_custom_call", output_to_operand_aliasing={{0}: (0, {})} | custom-call | tf_op jit(solution)/shard_map/finish/pallas_call | solution.py:339
  (25 shorter events, 10.4 us)
Async XLA Ops:
  0.6 21.3 %copy-start = (s32[1,1,8,2]{2,3,1,0:T(2,128)S(1)}, s32[1,1,8,2]{2,3,1,0:T(2,128)}, u32[]{:S(2)}) copy-start(s32[1,1,8,2]{2,3,1,0:T(2,128)} %param.8) | copy-start | bytes 196
  1.8 20.1 %collective-permute-start.1 = (f32[2,512,128]{2,1,0:T(8,128)S(1)}, f32[2,512,128]{2,1,0:T(8,128)S(1)}, u32[]{:S(2)}, u32[]{:S(2)}) collective-permute-start(f32[2,512,128]{2,1,0:T(8,128)S(1)} %get-tuple-element.28), channel_id=1, source_target_pairs={{16,0},{32,16},{48,32},{64,48},{80,64},{96,80},{112,96},{128,112},... | collective-permute-start | bytes 1572872 | tf_op jit(solution)/shard_map/ppermute | solution.py:24
  10.6 11.3 %collective-permute-start = (f32[2,128,256]{2,1,0:T(8,128)S(1)}, f32[2,128,256]{2,1,0:T(8,128)S(1)}, u32[]{:S(2)}, u32[]{:S(2)}) collective-permute-start(f32[2,128,256]{2,1,0:T(8,128)S(1)} %get-tuple-element.27), channel_id=1, source_target_pairs={{1,0},{2,1},{3,2},{4,3},{5,4},{6,5},{7,6},{8,7},{9,8},{10,9},{11,1... | collective-permute-start | bytes 786440 | tf_op jit(solution)/shard_map/ppermute | solution.py:20
  11.9 7.3 %collective-permute-start.2 = (f32[2,128,128]{2,1,0:T(8,128)S(1)}, f32[2,128,128]{2,1,0:T(8,128)S(1)}, u32[]{:S(2)}, u32[]{:S(2)}) collective-permute-start(f32[2,128,128]{2,1,0:T(8,128)S(1)} %get-tuple-element.29), channel_id=1, source_target_pairs={{17,0},{33,16},{49,32},{65,48},{81,64},{97,80},{113,96},{129,112},... | collective-permute-start | bytes 393224 | tf_op jit(solution)/shard_map/ppermute | solution.py:33
  25.7 23.2 %collective-permute-start.5 = (f32[2,3,128,128]{3,2,1,0:T(8,128)S(1)}, f32[2,3,128,128]{3,2,1,0:T(8,128)S(1)}, u32[]{:S(2)}, u32[]{:S(2)}) collective-permute-start(f32[2,3,128,128]{3,2,1,0:T(8,128)S(1)} %get-tuple-element.37), channel_id=1, source_target_pairs={{0,1},{1,2},{2,3},{3,4},{4,5},{5,6},{6,7},{7,8},{8,9},{9,10},{10,1... | collective-permute-start | bytes 1179656 | tf_op jit(solution)/shard_map/ppermute | solution.py:20
  30.0 19.0 %collective-permute-start.6 = (f32[2,3,128,128]{3,2,1,0:T(8,128)S(1)}, f32[2,3,128,128]{3,2,1,0:T(8,128)S(1)}, u32[]{:S(2)}, u32[]{:S(2)}) collective-permute-start(f32[2,3,128,128]{3,2,1,0:T(8,128)S(1)} %get-tuple-element.38), channel_id=1, source_target_pairs={{1,0},{2,1},{3,2},{4,3},{5,4},{6,5},{7,6},{8,7},{9,8},{10,9},{11,1... | collective-permute-start | bytes 1179656 | tf_op jit(solution)/shard_map/ppermute | solution.py:20
  31.3 74.6 %collective-permute-start.4 = (f32[2,640,128]{2,1,0:T(8,128)S(1)}, f32[2,640,128]{2,1,0:T(8,128)S(1)}, u32[]{:S(2)}, u32[]{:S(2)}) collective-permute-start(f32[2,640,128]{2,1,0:T(8,128)S(1)} %get-tuple-element.34.acc_0), channel_id=1, source_target_pairs={{16,0},{32,16},{48,32},{64,48},{80,64},{96,80},{112,96},{128,112},... | collective-permute-start | bytes 1966088 | tf_op jit(solution)/shard_map/ppermute | solution.py:24
  33.2 72.6 %collective-permute-start.3 = (f32[2,640,128]{2,1,0:T(8,128)S(1)}, f32[2,640,128]{2,1,0:T(8,128)S(1)}, u32[]{:S(2)}, u32[]{:S(2)}) collective-permute-start(f32[2,640,128]{2,1,0:T(8,128)S(1)} %get-tuple-element.36.acc_2), channel_id=1, source_target_pairs={{0,16},{16,32},{32,48},{48,64},{64,80},{80,96},{96,112},{112,128},... | collective-permute-start | bytes 1966088 | tf_op jit(solution)/shard_map/ppermute | solution.py:24
  49.0 56.8 %collective-permute-start.7 = (f32[2,2,128,128]{3,2,1,0:T(8,128)S(1)}, f32[2,2,128,128]{3,2,1,0:T(8,128)S(1)}, u32[]{:S(2)}, u32[]{:S(2)}) collective-permute-start(f32[2,2,128,128]{3,2,1,0:T(8,128)S(1)} %get-tuple-element.40), channel_id=1, source_target_pairs={{0,16},{16,32},{32,48},{48,64},{64,80},{80,96},{96,112},{112,128},... | collective-permute-start | bytes 786440 | tf_op jit(solution)/shard_map/ppermute | solution.py:24
  55.0 50.8 %collective-permute-start.8 = (f32[2,2,128,128]{3,2,1,0:T(8,128)S(1)}, f32[2,2,128,128]{3,2,1,0:T(8,128)S(1)}, u32[]{:S(2)}, u32[]{:S(2)}) collective-permute-start(f32[2,2,128,128]{3,2,1,0:T(8,128)S(1)} %get-tuple-element.41), channel_id=1, source_target_pairs={{16,0},{32,16},{48,32},{64,48},{80,64},{96,80},{112,96},{128,112},... | collective-permute-start | bytes 786440 | tf_op jit(solution)/shard_map/ppermute | solution.py:24
  112.1 54.8 %collective-permute-start.9 = (f32[2,512,128]{2,1,0:T(8,128)}, f32[2,512,128]{2,1,0:T(8,128)S(1)}, u32[]{:S(2)}, u32[]{:S(2)}) collective-permute-start(f32[2,512,128]{2,1,0:T(8,128)} %get-tuple-element.46), channel_id=1, source_target_pairs={{0,16},{16,32},{32,48},{48,64},{64,80},{80,96},{96,112},{112,128},... | collective-permute-start | bytes 1572872 | tf_op jit(solution)/shard_map/ppermute | solution.py:24
  115.0 12.0 %all-to-all-start.4 = ((f32[32,8,128]{2,1,0:T(8,128)}), f32[32,8,128]{2,1,0:T(8,128)S(1)}, u32[]{:S(2)}, u32[]{:S(2)}) async-start(f32[32,8,128]{2,1,0:T(8,128)} %bitcast.17), calls=%async_computation.4 | async-start | bytes 262144 | tf_op jit(solution)/shard_map/all_to_all | solution.py:37
  119.5 39.9 %collective-permute-start.10 = (f32[2,2,128,128]{3,2,1,0:T(8,128)}, f32[2,2,128,128]{3,2,1,0:T(8,128)S(1)}, u32[]{:S(2)}, u32[]{:S(2)}) collective-permute-start(f32[2,2,128,128]{3,2,1,0:T(8,128)} %get-tuple-element.47), channel_id=1, source_target_pairs={{0,1},{1,2},{2,3},{3,4},{4,5},{5,6},{6,7},{7,8},{8,9},{9,10},{10,1... | collective-permute-start | bytes 786440 | tf_op jit(solution)/shard_map/ppermute | solution.py:20
  135.0 16.6 %all-to-all-start.6 = ((f32[4,8,128]{2,1,0:T(8,128)}), f32[4,8,128]{2,1,0:T(8,128)S(1)}, u32[]{:S(2)}, u32[]{:S(2)}) async-start(f32[4,8,128]{2,1,0:T(8,128)} %fold_near.3), calls=%async_computation.6 | async-start | bytes 32768 | tf_op jit(solution)/shard_map/all_to_all | solution.py:37
  140.1 19.3 %collective-permute-start.11 = (f32[2,128,128]{2,1,0:T(8,128)}, f32[2,128,128]{2,1,0:T(8,128)S(1)}, u32[]{:S(2)}, u32[]{:S(2)}) collective-permute-start(f32[2,128,128]{2,1,0:T(8,128)} %get-tuple-element.48), channel_id=1, source_target_pairs={{0,17},{16,33},{32,49},{48,65},{64,81},{80,97},{96,113},{112,129},... | collective-permute-start | bytes 393224 | tf_op jit(solution)/shard_map/ppermute | solution.py:33
  152.3 14.6 %all-to-all-start.7 = ((f32[32,8,128]{2,1,0:T(8,128)}), f32[32,8,128]{2,1,0:T(8,128)S(1)}, u32[]{:S(2)}, u32[]{:S(2)}) async-start(f32[32,8,128]{2,1,0:T(8,128)} %fold_far.3), calls=%async_computation.7 | async-start | bytes 262144 | tf_op jit(solution)/shard_map/all_to_all | solution.py:37

commit v2 on v1

--- a/solution.py
+++ b/solution.py
@@ -33,6 +33,35 @@
     return lax.ppermute(value, ("tx", "ty"), pairs)
 
 
+def trade(value, axis, first):
+    size = lax.axis_size(axis)
+    pairs = []
+    for one in range(first, size - 1, 2):
+        pairs += [(one, one + 1), (one + 1, one)]
+    return lax.ppermute(value, axis, pairs)
+
+
+def gate_kernel(*refs):
+    pass
+
+
+def gate(values, after, far):
+    whole = pl.BlockSpec(memory_space=pltpu.HBM if far else pl.ANY)
+    if far:
+        values = [pltpu.with_memory_space_constraint(value, pltpu.HBM) for value in values]
+    return pl.pallas_call(
+        gate_kernel,
+        out_shape=[
+            (pltpu.HBM if far else jax.ShapeDtypeStruct)(value.shape, value.dtype)
+            for value in values
+        ],
+        in_specs=[whole] * len(values) + [pl.BlockSpec(memory_space=pl.ANY)],
+        out_specs=[whole] * len(values),
+        input_output_aliases={at: at for at in range(len(values))},
+        name="gate",
+    )(*values, after)
+
+
 def swap(parts, axes, groups):
     return lax.all_to_all(parts, axes, 0, 0, axis_index_groups=groups, tiled=True)
 
@@ -65,8 +94,11 @@
 def sum_along(parts):
     plane, near, far = device_groups()
     parts = fold(swap(parts, "tx", near), len(far[0]), "fold_near")
-    parts = fold(swap(parts, "tx", far), len(plane[0]), "fold_far")
-    parts = swap(parts, ("tx", "ty"), plane)
+    return fold(swap(parts, "tx", far), len(plane[0]), "fold_far")
+
+
+def collect(parts):
+    parts = swap(parts, ("tx", "ty"), device_groups()[0])
     return parts.reshape(2, -1, parts.shape[-1])
 
 
@@ -223,40 +255,51 @@
     wait(rest + copies.start((inten, inten_out)))
 
 
+def partners(odd, n, bottom):
+    block_a = jnp.where(odd[0] == 0, n, 0)
+    row_c = pl.multiple_of(jnp.where(odd[1] == 0, bottom, 0), 128)
+    return block_a, n - block_a, row_c, pl.multiple_of(bottom - row_c, 128)
+
+
 def first_kernel(
-    org, counts, ext_in, below, right, corner, probe, inten, table,
-    ext, acc_0, acc_1, acc_2, up, down, total, acc, sems,
+    org, counts, odd, ext_in, below, right, corner, probe, inten, table,
+    ext, side_a, side_b, inner, rows_c, rows_d, total, acc, sems,
 ):
     n = ext.shape[1] - 1
     width = ext.shape[3]
     bottom = ext.shape[2] - width
     for p in range(2):
         for j in range(n):
+            ext[p, j, :bottom] = ext_in[p, j, :bottom]
             ext[p, j, bottom:] = below[p, :, j * width : (j + 1) * width]
         ext[p, n, :bottom] = right[p]
         ext[p, n, bottom:] = corner[p]
     acc[...] = jnp.zeros_like(acc)
     total[...] = jnp.zeros_like(total)
     add_slots(org, counts[0], ext, acc, probe[0], probe[1], total, inten, table)
-    for p in range(2):
-        for j, part in enumerate((acc_0, acc_1, acc_2)):
-            part[p] = acc[p, j]
-            up[p, j] = acc[p, j, :width]
-            down[p, j] = acc[p, j, bottom:]
-
-
-def corners_kernel(from_up, from_down, after, to_left, to_right, sems):
+    block_a, block_b, row_c, row_d = partners(odd, n, bottom)
+    for p in range(2):
+        side_a[p] = acc[p, block_a]
+        side_b[p] = acc[p, block_b]
+        inner[p] = acc[p, 1]
+        for j in range(n + 1):
+            rows_c[p, j] = acc[p, j, pl.ds(row_c, width), :]
+            rows_d[p, j] = acc[p, j, pl.ds(row_d, width), :]
+
+
+def corners_kernel(odd, from_c, from_d, after, to_a, to_b, sems):
     del after
-    last = from_up.shape[1] - 1
-    for p in range(2):
-        for at, block in enumerate((from_up, from_down)):
-            to_left[p, at] = block[p, 0]
-            to_right[p, at] = block[p, last]
+    n = from_c.shape[1] - 1
+    block_a, block_b, _, _ = partners(odd, n, 0)
+    for p in range(2):
+        for at, block in enumerate((from_c, from_d)):
+            to_a[p, at] = block[p, block_a]
+            to_b[p, at] = block[p, block_b]
 
 
 def second_kernel(
-    org, counts, ext, acc_0, acc_1, acc_2, from_left, from_right, from_up, from_down,
-    more_left, more_right, probe_in, gathered, share, inten_in, table_in,
+    org, counts, odd, ext, side_a, side_b, inner, from_a, from_b, from_c, from_d,
+    more_a, more_b, probe_in, gathered, share, inten_in, table_in,
     obj_out, side_out, probe_out, total_out, right_out, down_out, corner_out,
     cur, acc, own, probe, total, inten, table, sems,
 ):
@@ -266,22 +309,19 @@
     copies = Copies(sems)
     loads = copies.start((inten_in, inten), (table_in, table))
     scale = peak_of(probe_in[0], probe_in[1])
-    mid = slice(width, bottom)
+    block_a, block_b, row_c, row_d = partners(odd, n, bottom)
+    where_c, where_d = pl.ds(row_c, width), pl.ds(row_d, width)
     for p in range(2):
         probe[p] = probe_in[p] - share[0] * gathered[p]
-        rows = ((slice(0, width), from_up, 0), (mid, None, 0), (slice(bottom, None), from_down, 1))
-        for j, (part, side, more) in enumerate(
-            ((acc_0, from_left, more_left), (acc_1, None, None), (acc_2, from_right, more_right))
-        ):
-            for where, edge, at in rows:
-                value = part[p, where]
-                if side is not None:
-                    value += side[p, where]
-                if edge is not None:
-                    value += edge[p, j]
-                    if more is not None:
-                        value += more[p, at]
-                cur[p, j, where] = ext[p, j, where] - scale * value
+        cur[p, 1] = ext[p, 1] - scale * inner[p]
+        cur[p, block_a] = ext[p, block_a] - scale * (side_a[p] + from_a[p])
+        cur[p, block_b] = ext[p, block_b] - scale * (side_b[p] + from_b[p])
+        for j in range(n + 1):
+            cur[p, j, where_c, :] -= scale * from_c[p, j]
+            cur[p, j, where_d, :] -= scale * from_d[p, j]
+        for block, more in ((block_a, more_a), (block_b, more_b)):
+            cur[p, block, where_c, :] -= scale * more[p, 0]
+            cur[p, block, where_d, :] -= scale * more[p, 1]
     acc[...] = jnp.zeros_like(acc)
     total[...] = jnp.zeros_like(total)
     wait(loads)
@@ -375,29 +415,34 @@
         prepare_kernel, "prepare", (), (0, 1, 2, 3, -5),
         [blocks, square, slots, kept, slots], [slots], 6, 4,
     )(object_planes, probe, inten, table)
-    ext, acc_0, acc_1, acc_2, up, down, total = call(
-        first_kernel, "first_pass", (0, 1), (), [blocks, tall, tall, tall, strip, strip, square],
-        [blocks], 1, 6, input_output_aliases={2: 0},
-    )(org, count, ext, below, right, corner, start, inten_near, table_near)
-    from_left, from_right = shift(acc_2, 0, 1), shift(acc_0, 0, -1)
-    from_up, from_down = shift(down, 1, 0), shift(up, -1, 0)
+    odd = jnp.stack([lax.axis_index("tx") % 2, lax.axis_index("ty") % 2]).astype(jnp.int32)
+    ext, side_a, side_b, inner, rows_c, rows_d, total = call(
+        first_kernel, "first_pass", (0, 1, 2), (),
+        [blocks, tall, tall, tall, strip, strip, square], [blocks], 1, 6,
+    )(org, count, odd, ext, below, right, corner, start, inten_near, table_near)
     parts = sum_in_plane(total)
-    to_left, to_right = call(
-        corners_kernel, "corners", (), (), [(2, 2, w, w)] * 2, [], 1, 1
-    )(from_up, from_down, parts)
-    more_left, more_right = shift(to_right, 0, 1), shift(to_left, 0, -1)
-    gathered = sum_along(parts)
+    side_a, side_b, rows_c, rows_d = gate((side_a, side_b, rows_c, rows_d), parts, False)
+    from_c, from_d = trade(rows_c, "ty", 0), trade(rows_d, "ty", 1)
+    from_a, from_b = trade(side_a, "tx", 0), trade(side_b, "tx", 1)
+    parts = sum_along(parts)
+    to_a, to_b = call(corners_kernel, "corners", (0,), (), [(2, 2, w, w)] * 2, [], 1, 1)(
+        odd, from_c, from_d, parts
+    )
+    more_a, more_b = trade(to_a, "tx", 0), trade(to_b, "tx", 1)
+    gathered = collect(parts)
     obj, side, current, total, to_right, to_down, to_corner = call(
-        second_kernel, "second_pass", (0, 1, 14), (15, 16, *range(-7, 0)),
+        second_kernel, "second_pass", (0, 1, 2, 15), (16, 17, *range(-7, 0)),
         [(2, rows, cols), (2, rows, w), square, square, (2, rows, w), (2, n, w, w), square],
         [blocks, blocks, (2, n, rows, w), square, square, slots, kept], n + 7, 9,
     )(
-        org, count, ext, acc_0, acc_1, acc_2, from_left, from_right, from_up, from_down,
-        more_left, more_right, start, gathered, share, inten, table,
-    )
+        org, count, odd, ext, side_a, side_b, inner, from_a, from_b, from_c, from_d,
+        more_a, more_b, start, gathered, share, inten, table,
+    )
+    parts = sum_along(sum_in_plane(total))
+    to_right, to_down, to_corner = gate((to_right, to_down, to_corner), parts, True)
     from_left, from_up = shift(to_right, 0, 1), shift(to_down, 1, 0)
     from_corner = shift(to_corner, 1, 1)
-    gathered = sum_along(sum_in_plane(total))
+    gathered = collect(parts)
     obj, current = call(
         final_kernel, "finish", (7,), (0, 1, 2, -1, -2), [(2, rows, cols), square],
         [(2, rows, w), (2, n - 1, w, w), square], 2 * n + 2, 3, input_output_aliases={0: 0},

time: 170 us -> 185 us (1.088)
  blocking collectives: 68.2 us -> 114 us
  waiting for transfers between devices: 25 us -> 5.23 us
  starting transfers between devices: 57.4 us -> 39.9 us
  local copies, waits for them, and re-layouts: 0.01 us -> 7.44 us
    all_to_all x5 -> x8, blocking collectives: 68.2 us -> 114 us  [swap(): lax.all_to_all(parts, axes, 0, 0, axis_index_groups=groups, tiled=True)]
    all_to_all x3 -> x0, waiting for transfers between devices: 19 us -> none  [swap(): lax.all_to_all(parts, axes, 0, 0, axis_index_groups=groups, tiled=True)]
    ppermute x0 -> x6, starting transfers between devices: none -> 18.2 us  [trade(): return lax.ppermute(value, axis, pairs)]
    all_to_all x3 -> x0, starting transfers between devices: 16.6 us -> none  [swap(): lax.all_to_all(parts, axes, 0, 0, axis_index_groups=groups, tiled=True)]
    ppermute x6 -> x2, starting transfers between devices: 25.2 us -> 14.5 us  [shift(): lax.ppermute(value, 'tx', [(b, b + cols) for b in range(n_c) if 0 <= b +...]
    unnamed x2 -> x24, local copies, waits for them, and re-layouts: 0.01 us -> 7.44 us
    ppermute x4 -> x2, starting transfers between devices: 10.1 us -> 3.31 us  [shift(): lax.ppermute(value, 'ty', [(a, a + rows) for a in range(n_r) if 0 <= a +...]
  transfers between devices with their start and end apart: 15 -> 12, of which waited for: 5 -> 2; matrix products, arithmetic and copies ran while one was open for 0% -> 0% of each run, Pallas kernels for 2% -> 1%
where the time goes in v2:
time: 185 us; the launch traced here: 184 us
  blocking collectives  114 us (62%)
  starting transfers between devices  39.9 us (22%)
  Pallas kernels  16.2 us (9%)
  local copies, waits for them, and re-layouts  7.44 us (4%)
  waiting for transfers between devices  5.23 us (3%)
    all_to_all x8, blocking collectives, swap(): lax.all_to_all(parts, axes, 0, 0, axis_index_groups=groups, tiled=True)  114 us
    ppermute x6, starting transfers between devices, trade(): return lax.ppermute(value, axis, pairs)  18.2 us
    pallas_call x12, Pallas kernels, run(): pl.pallas_call(kernel, out_shape=[space(s, F32) if isinstance(s, tuple) e...  16.2 us
    ppermute x2, starting transfers between devices, shift(): lax.ppermute(value, 'tx', [(b, b + cols) for b in range(n_c) if 0 <= b +...  14.5 us
    unnamed x24, local copies, waits for them, and re-layouts  7.44 us
    ppermute x2, starting transfers between devices, shift(): return lax.ppermute(value, ('tx', 'ty'), pairs)  3.79 us
  transfers between devices with their start and end apart: 12, of which 2 were waited for; matrix products, arithmetic and copies ran while one was open for 0% of the time, Pallas kernels for 1%

profile of v2, /device:TPU:1, one launch (start us, length us, event | category | flops | bytes accessed | tf_op | source)
XLA Modules:
  0.0 184.3 jit_solution(17597909791938025403)
XLA Ops:
  1.8 8.8 %collective-permute-start.1 = (f32[2,512,128]{2,1,0:T(8,128)S(1)}, f32[2,512,128]{2,1,0:T(8,128)S(1)}, u32[]{:S(2)}, u32[]{:S(2)}) collective-permute-start(f32[2,512,128]{2,1,0:T(8,128)S(1)} %get-tuple-element.35), channel_id=1, source_target_pairs={{16,0},{32,16},{48,32},{64,48},{80,64},{96,80},{112,96},{128,112},... | collective-permute-start | bytes 1572872 | tf_op jit(solution)/shard_map/ppermute | solution.py:24
  10.6 1.3 collective-permute-start
  13.9 2.1 %prepare.1 = (f32[2,3,640,128]{3,2,1,0:T(8,128)S(1)}, f32[2,128,128]{2,1,0:T(8,128)S(1)}, f32[8,128,128]{2,1,0:T(8,128)S(1)}, bf16[768,256]{1,0:T(8,128)(2,1)S(1)}, f32[8,128,128]{2,1,0:T(8,128)}) custom-call(f32[2,512,256]{2,1,0:T(8,128)} %tile.3, f32[2,128,128]{2,1,0:T(8,128)} %probe_in.1, f32[8,128,128]{2,1,0:T(8,128)} %bitcast.18, ...), custom_call_target="tpu_custom_call" | custom-call | tf_op jit(solution)/shard_map/prepare/pallas_call | solution.py:379
  16.1 3.1 %collective-permute-done.2.corner = f32[2,128,128]{2,1,0:T(8,128)S(1)} collective-permute-done((f32[2,128,128]{2,1,0:T(8,128)S(1)}, f32[2,128,128]{2,1,0:T(8,128)S(1)}, u32[]{:S(2)}, u32[]{:S(2)}) %collective-permute-start.2) | collective-permute-done | bytes 131104 | tf_op jit(solution)/shard_map/ppermute | solution.py:33
  19.9 2.1 %collective-permute-done.below = f32[2,128,256]{2,1,0:T(8,128)S(1)} collective-permute-done((f32[2,128,256]{2,1,0:T(8,128)S(1)}, f32[2,128,256]{2,1,0:T(8,128)S(1)}, u32[]{:S(2)}, u32[]{:S(2)}) %collective-permute-start) | collective-permute-done | bytes 262176 | tf_op jit(solution)/shard_map/ppermute | solution.py:20
  22.8 3.9 %first_pass.1 = (f32[2,3,640,128]{3,2,1,0:T(8,128)S(1)}, f32[2,640,128]{2,1,0:T(8,128)S(1)}, f32[2,640,128]{2,1,0:T(8,128)S(1)}, f32[2,640,128]{2,1,0:T(8,128)S(...) custom-call(s32[2,8]{1,0:T(2,128)S(1)} %bitcast.16, ...), custom_call_target="tpu_custom_call" | custom-call | tf_op jit(solution)/shard_map/first_pass/pallas_call | solution.py:379
  29.2 15.0 %all_to_all.40.parts = f32[32,8,128]{2,1,0:T(8,128)S(1)} all-to-all(f32[32,8,128]{2,1,0:T(8,128)S(1)} %bitcast.15), channel_id=1, replica_groups={{0,1,2,3,4,5,6,7,8,9,10,11,12,13,14,15,16,17,18,19,20,21,22,23,24,25,26..., dimensions={0} | all-to-all | bytes 262144 | tf_op jit(solution)/shard_map/all_to_all | solution.py:66
  44.9 2.1 %collective-permute-start.5 = (f32[2,3,128,128]{3,2,1,0:T(8,128)}, f32[2,3,128,128]{3,2,1,0:T(8,128)S(1)}, u32[]{:S(2)}, u32[]{:S(2)}) collective-permute-start(f32[2,3,128,128]{3,2,1,0:T(8,128)} %get-tuple-element.49), channel_id=1, source_target_pairs={{0,1},{1,0},{2,3},{3,2},{4,5},{5,4},{6,7},{7,6},{8,9},{9,8},{10,11... | collective-permute-start | bytes 1179656 | tf_op jit(solution)/shard_map/ppermute | solution.py:41
  47.7 2.8 %collective-permute-start.3 = (f32[2,640,128]{2,1,0:T(8,128)}, f32[2,640,128]{2,1,0:T(8,128)S(1)}, u32[]{:S(2)}, u32[]{:S(2)}) collective-permute-start(f32[2,640,128]{2,1,0:T(8,128)} %get-tuple-element.46.side_a), channel_id=1, source_target_pairs={{0,16},{16,0},{32,48},{48,32},{64,80},{80,64},{96,112},{112,96},{1... | collective-permute-start | bytes 1966088 | tf_op jit(solution)/shard_map/ppermute | solution.py:41
  50.5 2.2 %collective-permute-start.4 = (f32[2,640,128]{2,1,0:T(8,128)}, f32[2,640,128]{2,1,0:T(8,128)S(1)}, u32[]{:S(2)}, u32[]{:S(2)}) collective-permute-start(f32[2,640,128]{2,1,0:T(8,128)} %get-tuple-element.47.side_b), channel_id=1, source_target_pairs={{16,32},{32,16},{48,64},{64,48},{80,96},{96,80},{112,128},{128,112... | collective-permute-start | bytes 1966088 | tf_op jit(solution)/shard_map/ppermute | solution.py:41
  52.7 11.2 %all_to_all.41.parts = f32[4,8,128]{2,1,0:T(8,128)S(1)} all-to-all(f32[4,8,128]{2,1,0:T(8,128)S(1)} %copy-done.8), channel_id=1, replica_groups={{0,32,64,96},{128,160,192,224},{256,288,320,352},{384,416,448,480},{16,..., dimensions={0} | all-to-all | bytes 32768 | tf_op jit(solution)/shard_map/all_to_all | solution.py:66
  63.9 21.8 %all_to_all.42.parts = f32[4,8,128]{2,1,0:T(8,128)S(1)} all-to-all(f32[4,8,128]{2,1,0:T(8,128)S(1)} %fold_near.2), channel_id=1, replica_groups={{0,128,256,384},{32,160,288,416},{64,192,320,448},{96,224,352,480},{16,..., dimensions={0} | all-to-all | bytes 32768 | tf_op jit(solution)/shard_map/all_to_all | solution.py:66
  86.3 8.3 %collective-permute-start.7 = (f32[2,2,128,128]{3,2,1,0:T(8,128)S(1)}, f32[2,2,128,128]{3,2,1,0:T(8,128)S(1)}, u32[]{:S(2)}, u32[]{:S(2)}) collective-permute-start(f32[2,2,128,128]{3,2,1,0:T(8,128)S(1)} %get-tuple-element.51), channel_id=1, source_target_pairs={{0,16},{16,0},{32,48},{48,32},{64,80},{80,64},{96,112},{112,96},{1... | collective-permute-start | bytes 786440 | tf_op jit(solution)/shard_map/ppermute | solution.py:41
  94.6 2.2 %collective-permute-start.8 = (f32[2,2,128,128]{3,2,1,0:T(8,128)S(1)}, f32[2,2,128,128]{3,2,1,0:T(8,128)S(1)}, u32[]{:S(2)}, u32[]{:S(2)}) collective-permute-start(f32[2,2,128,128]{3,2,1,0:T(8,128)S(1)} %get-tuple-element.52), channel_id=1, source_target_pairs={{16,32},{32,16},{48,64},{64,48},{80,96},{96,80},{112,128},{128,112... | collective-permute-start | bytes 786440 | tf_op jit(solution)/shard_map/ppermute | solution.py:41
  96.8 14.7 %all_to_all.43 = f32[32,8,128]{2,1,0:T(8,128)S(1)} all-to-all(f32[32,8,128]{2,1,0:T(8,128)S(1)} %fold_far.2.after), channel_id=1, replica_groups={{0,1,2,3,4,5,6,7,8,9,10,11,12,13,14,15,16,17,18,19,20,21,22,23,24,25,26..., dimensions={0} | all-to-all | bytes 262144 | tf_op jit(solution)/shard_map/all_to_all | solution.py:66
  113.7 6.2 %second_pass.1 = (f32[2,512,256]{2,1,0:T(8,128)}, f32[2,512,128]{2,1,0:T(8,128)}, f32[2,128,128]{2,1,0:T(8,128)}, f32[2,128,128]{2,1,0:T(8,128)}, f32[2,512,128]...) custom-call(s32[2,8]{1,0:T(2,128)S(1)} %bitcast.17, s32[1]{0:T(128)} %bitcast.12.counts, ...), custom_call_target="tpu_custom_call" | custom-call | tf_op jit(solution)/shard_map/second_pass/pallas_call | solution.py:379
  119.9 13.1 %all_to_all.44.parts = f32[32,8,128]{2,1,0:T(8,128)S(1)} all-to-all(f32[32,8,128]{2,1,0:T(8,128)} %bitcast.19), channel_id=1, replica_groups={{0,1,2,3,4,5,6,7,8,9,10,11,12,13,14,15,16,17,18,19,20,21,22,23,24,25,26..., dimensions={0} | all-to-all | bytes 262144 | tf_op jit(solution)/shard_map/all_to_all | solution.py:66
  133.0 7.9 %all_to_all.45.parts = f32[4,8,128]{2,1,0:T(8,128)S(1)} all-to-all(f32[4,8,128]{2,1,0:T(8,128)S(1)} %fold_plane.3), channel_id=1, replica_groups={{0,32,64,96},{128,160,192,224},{256,288,320,352},{384,416,448,480},{16,..., dimensions={0} | all-to-all | bytes 32768 | tf_op jit(solution)/shard_map/all_to_all | solution.py:66
  140.9 16.0 %all_to_all.46.parts = f32[4,8,128]{2,1,0:T(8,128)S(1)} all-to-all(f32[4,8,128]{2,1,0:T(8,128)S(1)} %fold_near.3), channel_id=1, replica_groups={{0,128,256,384},{32,160,288,416},{64,192,320,448},{96,224,352,480},{16,..., dimensions={0} | all-to-all | bytes 32768 | tf_op jit(solution)/shard_map/all_to_all | solution.py:66
  157.6 5.8 %collective-permute-start.9 = (f32[2,512,128]{2,1,0:T(8,128)}, f32[2,512,128]{2,1,0:T(8,128)S(1)}, u32[]{:S(2)}, u32[]{:S(2)}) collective-permute-start(f32[2,512,128]{2,1,0:T(8,128)} %get-tuple-element.61), channel_id=1, source_target_pairs={{0,16},{16,32},{32,48},{48,64},{64,80},{80,96},{96,112},{112,128},... | collective-permute-start | bytes 1572872 | tf_op jit(solution)/shard_map/ppermute | solution.py:24
  163.4 2.0 %collective-permute-start.10 = (f32[2,2,128,128]{3,2,1,0:T(8,128)}, f32[2,2,128,128]{3,2,1,0:T(8,128)S(1)}, u32[]{:S(2)}, u32[]{:S(2)}) collective-permute-start(f32[2,2,128,128]{3,2,1,0:T(8,128)} %get-tuple-element.62), channel_id=1, source_target_pairs={{0,1},{1,2},{2,3},{3,4},{4,5},{5,6},{6,7},{7,8},{8,9},{9,10},{10,1... | collective-permute-start | bytes 786440 | tf_op jit(solution)/shard_map/ppermute | solution.py:20
  165.4 2.5 %collective-permute-start.11 = (f32[2,128,128]{2,1,0:T(8,128)}, f32[2,128,128]{2,1,0:T(8,128)S(1)}, u32[]{:S(2)}, u32[]{:S(2)}) collective-permute-start(f32[2,128,128]{2,1,0:T(8,128)} %get-tuple-element.63), channel_id=1, source_target_pairs={{0,17},{16,33},{32,49},{48,65},{64,81},{80,97},{96,113},{112,129},... | collective-permute-start | bytes 393224 | tf_op jit(solution)/shard_map/ppermute | solution.py:33
  167.9 14.2 %all_to_all.47 = f32[32,8,128]{2,1,0:T(8,128)S(1)} all-to-all(f32[32,8,128]{2,1,0:T(8,128)} %copy-done.4), channel_id=1, replica_groups={{0,1,2,3,4,5,6,7,8,9,10,11,12,13,14,15,16,17,18,19,20,21,22,23,24,25,26..., dimensions={0} | all-to-all | bytes 262144 | tf_op jit(solution)/shard_map/all_to_all | solution.py:66
  182.2 2.1 %finish.1 = (f32[2,512,256]{2,1,0:T(8,128)}, f32[2,128,128]{2,1,0:T(8,128)}) custom-call(f32[2,512,256]{2,1,0:T(8,128)} %get-tuple-element.54.obj_in, f32[2,512,128]{2,1,0:T(8,128)} %get-tuple-element.55.side_in, f32[2,128,128]{2,1,0:T(8,128)} %get-tuple-element.56.probe_in, ...), custom_call_target="tpu_custom_call", output_to_operand_aliasing={{0}: (0, {})} | custom-call | tf_op jit(solution)/shard_map/finish/pallas_call | solution.py:379
  (47 shorter events, 11.4 us)
Async XLA Ops:
  0.6 21.3 %copy-start.11 = (s32[1,1,8,2]{2,3,1,0:T(2,128)S(1)}, s32[1,1,8,2]{2,3,1,0:T(2,128)}, u32[]{:S(2)}) copy-start(s32[1,1,8,2]{2,3,1,0:T(2,128)} %param.8) | copy-start | bytes 196
  1.8 20.1 %collective-permute-start.1 = (f32[2,512,128]{2,1,0:T(8,128)S(1)}, f32[2,512,128]{2,1,0:T(8,128)S(1)}, u32[]{:S(2)}, u32[]{:S(2)}) collective-permute-start(f32[2,512,128]{2,1,0:T(8,128)S(1)} %get-tuple-element.35), channel_id=1, source_target_pairs={{16,0},{32,16},{48,32},{64,48},{80,64},{96,80},{112,96},{128,112},... | collective-permute-start | bytes 1572872 | tf_op jit(solution)/shard_map/ppermute | solution.py:24
  10.6 11.3 %collective-permute-start = (f32[2,128,256]{2,1,0:T(8,128)S(1)}, f32[2,128,256]{2,1,0:T(8,128)S(1)}, u32[]{:S(2)}, u32[]{:S(2)}) collective-permute-start(f32[2,128,256]{2,1,0:T(8,128)S(1)} %get-tuple-element.34), channel_id=1, source_target_pairs={{1,0},{2,1},{3,2},{4,3},{5,4},{6,5},{7,6},{8,7},{9,8},{10,9},{11,1... | collective-permute-start | bytes 786440 | tf_op jit(solution)/shard_map/ppermute | solution.py:20
  11.9 7.3 %collective-permute-start.2 = (f32[2,128,128]{2,1,0:T(8,128)S(1)}, f32[2,128,128]{2,1,0:T(8,128)S(1)}, u32[]{:S(2)}, u32[]{:S(2)}) collective-permute-start(f32[2,128,128]{2,1,0:T(8,128)S(1)} %get-tuple-element.36), channel_id=1, source_target_pairs={{17,0},{33,16},{49,32},{65,48},{81,64},{97,80},{113,96},{129,112},... | collective-permute-start | bytes 393224 | tf_op jit(solution)/shard_map/ppermute | solution.py:33
  19.2 0.7 copy-start.9
  21.9 0.9 copy-start.10
  26.7 0.8 copy-start
  27.6 0.8 copy-start.2
  28.4 0.8 copy-start.6
  29.2 15.1 %copy-start.5 = (f32[2,3,128,128]{3,2,1,0:T(8,128)}, f32[2,3,128,128]{3,2,1,0:T(8,128)S(1)}, u32[]{:S(2)}) copy-start(f32[2,3,128,128]{3,2,1,0:T(8,128)S(1)} %get-tuple-element.43.refs_2_) | copy-start | bytes 1179652
  44.3 0.6 copy-start.7
  44.9 7.8 %copy-start.8 = (f32[4,8,128]{2,1,0:T(8,128)S(1)}, f32[4,8,128]{2,1,0:T(8,128)}, u32[]{:S(2)}) copy-start(f32[4,8,128]{2,1,0:T(8,128)} %copy-done.7) | copy-start | bytes 49156
  44.9 40.8 %collective-permute-start.5 = (f32[2,3,128,128]{3,2,1,0:T(8,128)}, f32[2,3,128,128]{3,2,1,0:T(8,128)S(1)}, u32[]{:S(2)}, u32[]{:S(2)}) collective-permute-start(f32[2,3,128,128]{3,2,1,0:T(8,128)} %get-tuple-element.49), channel_id=1, source_target_pairs={{0,1},{1,0},{2,3},{3,2},{4,5},{5,4},{6,7},{7,6},{8,9},{9,8},{10,11... | collective-permute-start | bytes 1179656 | tf_op jit(solution)/shard_map/ppermute | solution.py:41
  47.0 38.7 %collective-permute-start.6 = (f32[2,3,128,128]{3,2,1,0:T(8,128)}, f32[2,3,128,128]{3,2,1,0:T(8,128)S(1)}, u32[]{:S(2)}, u32[]{:S(2)}) collective-permute-start(f32[2,3,128,128]{3,2,1,0:T(8,128)} %get-tuple-element.50), channel_id=1, source_target_pairs={{1,2},{2,1},{3,4},{4,3},{5,6},{6,5},{7,8},{8,7},{9,10},{10,9},{11,... | collective-permute-start | bytes 1179656 | tf_op jit(solution)/shard_map/ppermute | solution.py:41
  47.7 63.8 %collective-permute-start.3 = (f32[2,640,128]{2,1,0:T(8,128)}, f32[2,640,128]{2,1,0:T(8,128)S(1)}, u32[]{:S(2)}, u32[]{:S(2)}) collective-permute-start(f32[2,640,128]{2,1,0:T(8,128)} %get-tuple-element.46.side_a), channel_id=1, source_target_pairs={{0,16},{16,0},{32,48},{48,32},{64,80},{80,64},{96,112},{112,96},{1... | collective-permute-start | bytes 1966088 | tf_op jit(solution)/shard_map/ppermute | solution.py:41
  50.5 61.1 %collective-permute-start.4 = (f32[2,640,128]{2,1,0:T(8,128)}, f32[2,640,128]{2,1,0:T(8,128)S(1)}, u32[]{:S(2)}, u32[]{:S(2)}) collective-permute-start(f32[2,640,128]{2,1,0:T(8,128)} %get-tuple-element.47.side_b), channel_id=1, source_target_pairs={{16,32},{32,16},{48,64},{64,48},{80,96},{96,80},{112,128},{128,112... | collective-permute-start | bytes 1966088 | tf_op jit(solution)/shard_map/ppermute | solution.py:41
  86.3 25.2 %collective-permute-start.7 = (f32[2,2,128,128]{3,2,1,0:T(8,128)S(1)}, f32[2,2,128,128]{3,2,1,0:T(8,128)S(1)}, u32[]{:S(2)}, u32[]{:S(2)}) collective-permute-start(f32[2,2,128,128]{3,2,1,0:T(8,128)S(1)} %get-tuple-element.51), channel_id=1, source_target_pairs={{0,16},{16,0},{32,48},{48,32},{64,80},{80,64},{96,112},{112,96},{1... | collective-permute-start | bytes 786440 | tf_op jit(solution)/shard_map/ppermute | solution.py:41
  94.6 16.9 %collective-permute-start.8 = (f32[2,2,128,128]{3,2,1,0:T(8,128)S(1)}, f32[2,2,128,128]{3,2,1,0:T(8,128)S(1)}, u32[]{:S(2)}, u32[]{:S(2)}) collective-permute-start(f32[2,2,128,128]{3,2,1,0:T(8,128)S(1)} %get-tuple-element.52), channel_id=1, source_target_pairs={{16,32},{32,16},{48,64},{64,48},{80,96},{96,80},{112,128},{128,112... | collective-permute-start | bytes 786440 | tf_op jit(solution)/shard_map/ppermute | solution.py:41
  111.5 1.1 copy-start.1
  112.6 1.1 copy-start.3
  156.9 0.7 copy-start.4
  157.6 24.5 %collective-permute-start.9 = (f32[2,512,128]{2,1,0:T(8,128)}, f32[2,512,128]{2,1,0:T(8,128)S(1)}, u32[]{:S(2)}, u32[]{:S(2)}) collective-permute-start(f32[2,512,128]{2,1,0:T(8,128)} %get-tuple-element.61), channel_id=1, source_target_pairs={{0,16},{16,32},{32,48},{48,64},{64,80},{80,96},{96,112},{112,128},... | collective-permute-start | bytes 1572872 | tf_op jit(solution)/shard_map/ppermute | solution.py:24
  163.4 18.8 %collective-permute-start.10 = (f32[2,2,128,128]{3,2,1,0:T(8,128)}, f32[2,2,128,128]{3,2,1,0:T(8,128)S(1)}, u32[]{:S(2)}, u32[]{:S(2)}) collective-permute-start(f32[2,2,128,128]{3,2,1,0:T(8,128)} %get-tuple-element.62), channel_id=1, source_target_pairs={{0,1},{1,2},{2,3},{3,4},{4,5},{5,6},{6,7},{7,8},{8,9},{9,10},{10,1... | collective-permute-start | bytes 786440 | tf_op jit(solution)/shard_map/ppermute | solution.py:20
  165.4 16.7 %collective-permute-start.11 = (f32[2,128,128]{2,1,0:T(8,128)}, f32[2,128,128]{2,1,0:T(8,128)S(1)}, u32[]{:S(2)}, u32[]{:S(2)}) collective-permute-start(f32[2,128,128]{2,1,0:T(8,128)} %get-tuple-element.63), channel_id=1, source_target_pairs={{0,17},{16,33},{32,49},{48,65},{64,81},{80,97},{96,113},{112,129},... | collective-permute-start | bytes 393224 | tf_op jit(solution)/shard_map/ppermute | solution.py:33

commit v3 on v1

--- a/solution.py
+++ b/solution.py
@@ -43,29 +43,18 @@
     plane = [
         [(z * CORES + c) * n_r + a for c in range(CORES) for a in range(n_r)] for z in range(depth)
     ]
-    near = min(4, depth)
-
-    def along(step, size):
-        return [
-            [(first + i * step) * CORES + c for i in range(size)]
-            for c in range(CORES)
-            for first in range(depth)
-            if first // step % size == 0
-        ]
-
-    return plane, along(1, near), along(near, depth // near)
+    return plane, [[z * CORES + c for z in range(depth)] for c in range(CORES)]
 
 
 def sum_in_plane(value):
-    plane, near, far = device_groups()
+    plane, line = device_groups()
     parts = value.reshape(len(plane[0]), -1, value.shape[-1])
-    return fold(swap(parts, ("tx", "ty"), plane), len(near[0]), "fold_plane")
+    return fold(swap(parts, ("tx", "ty"), plane), len(line[0]), "fold_plane")
 
 
 def sum_along(parts):
-    plane, near, far = device_groups()
-    parts = fold(swap(parts, "tx", near), len(far[0]), "fold_near")
-    parts = fold(swap(parts, "tx", far), len(plane[0]), "fold_far")
+    plane, line = device_groups()
+    parts = fold(swap(parts, "tx", line), len(plane[0]), "fold_line")
     parts = swap(parts, ("tx", "ty"), plane)
     return parts.reshape(2, -1, parts.shape[-1])
 
@@ -225,13 +214,14 @@
 
 def first_kernel(
     org, counts, ext_in, below, right, corner, probe, inten, table,
-    ext, acc_0, acc_1, acc_2, up, down, total, acc, sems,
+    ext, acc_0, acc_1, acc_2, total, acc, sems,
 ):
     n = ext.shape[1] - 1
     width = ext.shape[3]
     bottom = ext.shape[2] - width
     for p in range(2):
         for j in range(n):
+            ext[p, j, :bottom] = ext_in[p, j, :bottom]
             ext[p, j, bottom:] = below[p, :, j * width : (j + 1) * width]
         ext[p, n, :bottom] = right[p]
         ext[p, n, bottom:] = corner[p]
@@ -241,22 +231,22 @@
     for p in range(2):
         for j, part in enumerate((acc_0, acc_1, acc_2)):
             part[p] = acc[p, j]
-            up[p, j] = acc[p, j, :width]
-            down[p, j] = acc[p, j, bottom:]
-
-
-def corners_kernel(from_up, from_down, after, to_left, to_right, sems):
+
+
+def strips_kernel(acc_0, acc_1, acc_2, from_left, from_right, after, up, down, sems):
     del after
-    last = from_up.shape[1] - 1
-    for p in range(2):
-        for at, block in enumerate((from_up, from_down)):
-            to_left[p, at] = block[p, 0]
-            to_right[p, at] = block[p, last]
+    width = up.shape[2]
+    bottom = acc_0.shape[1] - width
+    for p in range(2):
+        for rows, block in ((slice(0, width), up), (slice(bottom, None), down)):
+            block[p, 0] = acc_0[p, rows] + from_left[p, rows]
+            block[p, 1] = acc_1[p, rows]
+            block[p, 2] = acc_2[p, rows] + from_right[p, rows]
 
 
 def second_kernel(
     org, counts, ext, acc_0, acc_1, acc_2, from_left, from_right, from_up, from_down,
-    more_left, more_right, probe_in, gathered, share, inten_in, table_in,
+    probe_in, gathered, share, inten_in, table_in,
     obj_out, side_out, probe_out, total_out, right_out, down_out, corner_out,
     cur, acc, own, probe, total, inten, table, sems,
 ):
@@ -269,18 +259,16 @@
     mid = slice(width, bottom)
     for p in range(2):
         probe[p] = probe_in[p] - share[0] * gathered[p]
-        rows = ((slice(0, width), from_up, 0), (mid, None, 0), (slice(bottom, None), from_down, 1))
-        for j, (part, side, more) in enumerate(
-            ((acc_0, from_left, more_left), (acc_1, None, None), (acc_2, from_right, more_right))
+        rows = ((slice(0, width), from_up), (mid, None), (slice(bottom, None), from_down))
+        for j, (part, side) in enumerate(
+            ((acc_0, from_left), (acc_1, None), (acc_2, from_right))
         ):
-            for where, edge, at in rows:
+            for where, edge in rows:
                 value = part[p, where]
                 if side is not None:
                     value += side[p, where]
                 if edge is not None:
                     value += edge[p, j]
-                    if more is not None:
-                        value += more[p, at]
                 cur[p, j, where] = ext[p, j, where] - scale * value
     acc[...] = jnp.zeros_like(acc)
     total[...] = jnp.zeros_like(total)
@@ -375,25 +363,23 @@
         prepare_kernel, "prepare", (), (0, 1, 2, 3, -5),
         [blocks, square, slots, kept, slots], [slots], 6, 4,
     )(object_planes, probe, inten, table)
-    ext, acc_0, acc_1, acc_2, up, down, total = call(
-        first_kernel, "first_pass", (0, 1), (), [blocks, tall, tall, tall, strip, strip, square],
-        [blocks], 1, 6, input_output_aliases={2: 0},
+    ext, acc_0, acc_1, acc_2, total = call(
+        first_kernel, "first_pass", (0, 1), (), [blocks, tall, tall, tall, square], [blocks], 1, 6
     )(org, count, ext, below, right, corner, start, inten_near, table_near)
     from_left, from_right = shift(acc_2, 0, 1), shift(acc_0, 0, -1)
+    parts = sum_in_plane(total)
+    up, down = call(strips_kernel, "strips", (), (), [strip, strip], [], 1, 1)(
+        acc_0, acc_1, acc_2, from_left, from_right, parts
+    )
     from_up, from_down = shift(down, 1, 0), shift(up, -1, 0)
-    parts = sum_in_plane(total)
-    to_left, to_right = call(
-        corners_kernel, "corners", (), (), [(2, 2, w, w)] * 2, [], 1, 1
-    )(from_up, from_down, parts)
-    more_left, more_right = shift(to_right, 0, 1), shift(to_left, 0, -1)
     gathered = sum_along(parts)
     obj, side, current, total, to_right, to_down, to_corner = call(
-        second_kernel, "second_pass", (0, 1, 14), (15, 16, *range(-7, 0)),
+        second_kernel, "second_pass", (0, 1, 12), (13, 14, *range(-7, 0)),
         [(2, rows, cols), (2, rows, w), square, square, (2, rows, w), (2, n, w, w), square],
         [blocks, blocks, (2, n, rows, w), square, square, slots, kept], n + 7, 9,
     )(
         org, count, ext, acc_0, acc_1, acc_2, from_left, from_right, from_up, from_down,
-        more_left, more_right, start, gathered, share, inten, table,
+        start, gathered, share, inten, table,
     )
     from_left, from_up = shift(to_right, 0, 1), shift(to_down, 1, 0)
     from_corner = shift(to_corner, 1, 1)

time: 170 us -> 148 us (0.87)
  starting transfers between devices: 57.4 us -> 39.6 us
  waiting for transfers between devices: 25 us -> 18.3 us
  blocking collectives: 68.2 us -> 71.2 us
    ppermute x6 -> x4, starting transfers between devices: 25.2 us -> 17.3 us  [shift(): lax.ppermute(value, 'tx', [(b, b + cols) for b in range(n_c) if 0 <= b +...]
    all_to_all x3 -> x2, starting transfers between devices: 16.6 us -> 9.47 us  [swap(): lax.all_to_all(parts, axes, 0, 0, axis_index_groups=groups, tiled=True)]
    all_to_all x3 -> x2, waiting for transfers between devices: 19 us -> 12.4 us  [swap(): lax.all_to_all(parts, axes, 0, 0, axis_index_groups=groups, tiled=True)]
    ppermute x4, starting transfers between devices: 10.1 us -> 6.66 us  [shift(): lax.ppermute(value, 'ty', [(a, a + rows) for a in range(n_r) if 0 <= a +...]
    all_to_all x5 -> x4, blocking collectives: 68.2 us -> 71.2 us  [swap(): lax.all_to_all(parts, axes, 0, 0, axis_index_groups=groups, tiled=True)]
    pallas_call x12 -> x10, Pallas kernels: 16.9 us -> 16.9 us  [run(): pl.pallas_call(kernel, out_shape=[space(s, F32) if isinstance(s, tuple) e...]
  transfers between devices with their start and end apart: 15 -> 12, of which waited for: 5 -> 4; matrix products, arithmetic and copies ran while one was open for 0% -> 0% of each run, Pallas kernels for 2% -> 2%
where the time goes in v3:
time: 148 us
  blocking collectives  71.2 us (48%)
  starting transfers between devices  39.6 us (27%)
  waiting for transfers between devices  18.3 us (12%)
  Pallas kernels  16.9 us (11%)
  between operations  1.49 us (1%)
    all_to_all x4, blocking collectives, swap(): lax.all_to_all(parts, axes, 0, 0, axis_index_groups=groups, tiled=True)  71.2 us
    ppermute x4, starting transfers between devices, shift(): lax.ppermute(value, 'tx', [(b, b + cols) for b in range(n_c) if 0 <= b +...  17.3 us
    pallas_call x10, Pallas kernels, run(): pl.pallas_call(kernel, out_shape=[space(s, F32) if isinstance(s, tuple) e...  16.9 us
    all_to_all x2, waiting for transfers between devices, swap(): lax.all_to_all(parts, axes, 0, 0, axis_index_groups=groups, tiled=True)  12.4 us
    all_to_all x2, starting transfers between devices, swap(): lax.all_to_all(parts, axes, 0, 0, axis_index_groups=groups, tiled=True)  9.47 us
    ppermute x4, starting transfers between devices, shift(): lax.ppermute(value, 'ty', [(a, a + rows) for a in range(n_r) if 0 <= a +...  6.66 us
    ppermute x2, starting transfers between devices, shift(): return lax.ppermute(value, ('tx', 'ty'), pairs)  6.14 us
    ppermute x2, waiting for transfers between devices, shift(): return lax.ppermute(value, ('tx', 'ty'), pairs)  3.24 us
  transfers between devices with their start and end apart: 12, of which 4 were waited for; matrix products, arithmetic and copies ran while one was open for 0% of the time, Pallas kernels for 2%

profile of v3, /device:TPU:1, one launch (start us, length us, event | category | flops | bytes accessed | tf_op | source)
XLA Modules:
  0.0 147.6 jit_solution(9149835047594747972)
XLA Ops:
  1.8 8.8 %collective-permute-start.1 = (f32[2,512,128]{2,1,0:T(8,128)S(1)}, f32[2,512,128]{2,1,0:T(8,128)S(1)}, u32[]{:S(2)}, u32[]{:S(2)}) collective-permute-start(f32[2,512,128]{2,1,0:T(8,128)S(1)} %get-tuple-element.26), channel_id=1, source_target_pairs={{16,0},{32,16},{48,32},{64,48},{80,64},{96,80},{112,96},{128,112},... | collective-permute-start | bytes 1572872 | tf_op jit(solution)/shard_map/ppermute | solution.py:24
  10.6 1.3 collective-permute-start
  11.9 1.3 collective-permute-start.2
  13.9 2.1 %prepare.1 = (f32[2,3,640,128]{3,2,1,0:T(8,128)S(1)}, f32[2,128,128]{2,1,0:T(8,128)S(1)}, f32[8,128,128]{2,1,0:T(8,128)S(1)}, bf16[768,256]{1,0:T(8,128)(2,1)S(1)}, f32[8,128,128]{2,1,0:T(8,128)}) custom-call(f32[2,512,256]{2,1,0:T(8,128)} %tile.3, f32[2,128,128]{2,1,0:T(8,128)} %probe_in.1, f32[8,128,128]{2,1,0:T(8,128)} %bitcast.16, ...), custom_call_target="tpu_custom_call" | custom-call | tf_op jit(solution)/shard_map/prepare/pallas_call | solution.py:327
  16.0 3.2 %collective-permute-done.2.corner = f32[2,128,128]{2,1,0:T(8,128)S(1)} collective-permute-done((f32[2,128,128]{2,1,0:T(8,128)S(1)}, f32[2,128,128]{2,1,0:T(8,128)S(1)}, u32[]{:S(2)}, u32[]{:S(2)}) %collective-permute-start.2) | collective-permute-done | bytes 131104 | tf_op jit(solution)/shard_map/ppermute | solution.py:33
  19.2 2.7 %collective-permute-done.below = f32[2,128,256]{2,1,0:T(8,128)S(1)} collective-permute-done((f32[2,128,256]{2,1,0:T(8,128)S(1)}, f32[2,128,256]{2,1,0:T(8,128)S(1)}, u32[]{:S(2)}, u32[]{:S(2)}) %collective-permute-start) | collective-permute-done | bytes 262176 | tf_op jit(solution)/shard_map/ppermute | solution.py:20
  21.9 3.8 %first_pass.1 = (f32[2,3,640,128]{3,2,1,0:T(8,128)S(1)}, f32[2,640,128]{2,1,0:T(8,128)S(1)}, f32[2,640,128]{2,1,0:T(8,128)S(1)}, f32[2,640,128]{2,1,0:T(8,128)S(1)}, f32[2,128,128]{2,1,0:T(8,128)S(1)}) custom-call(s32[2,8]{1,0:T(2,128)S(1)} %bitcast.14, s32[1]{0:T(128)} %bitcast.9.counts, f32[2,3,640,128]{3,2,1,0:T(8,128)S(1)} %get-tuple-element.24.ext_in, ...), custom_call_target="tpu_custom_call" | custom-call | tf_op jit(solution)/shard_map/first_pass/pallas_call | solution.py:327
  25.8 2.4 %collective-permute-start.4 = (f32[2,640,128]{2,1,0:T(8,128)S(1)}, f32[2,640,128]{2,1,0:T(8,128)S(1)}, u32[]{:S(2)}, u32[]{:S(2)}) collective-permute-start(f32[2,640,128]{2,1,0:T(8,128)S(1)} %get-tuple-element.32.acc_0), channel_id=1, source_target_pairs={{16,0},{32,16},{48,32},{64,48},{80,64},{96,80},{112,96},{128,112},... | collective-permute-start | bytes 1966088 | tf_op jit(solution)/shard_map/ppermute | solution.py:24
  28.2 3.1 %collective-permute-start.3 = (f32[2,640,128]{2,1,0:T(8,128)S(1)}, f32[2,640,128]{2,1,0:T(8,128)S(1)}, u32[]{:S(2)}, u32[]{:S(2)}) collective-permute-start(f32[2,640,128]{2,1,0:T(8,128)S(1)} %get-tuple-element.34.acc_2), channel_id=1, source_target_pairs={{0,16},{16,32},{32,48},{48,64},{64,80},{80,96},{96,112},{112,128},... | collective-permute-start | bytes 1966088 | tf_op jit(solution)/shard_map/ppermute | solution.py:24
  31.3 12.5 %all_to_all.30.parts = f32[32,8,128]{2,1,0:T(8,128)S(1)} all-to-all(f32[32,8,128]{2,1,0:T(8,128)S(1)} %bitcast.13), channel_id=1, replica_groups={{0,1,2,3,4,5,6,7,8,9,10,11,12,13,14,15,16,17,18,19,20,21,22,23,24,25,26..., dimensions={0} | all-to-all | bytes 262144 | tf_op jit(solution)/shard_map/all_to_all | solution.py:37
  44.0 2.0 %collective-permute-start.5 = (f32[2,3,128,128]{3,2,1,0:T(8,128)S(1)}, f32[2,3,128,128]{3,2,1,0:T(8,128)S(1)}, u32[]{:S(2)}, u32[]{:S(2)}) collective-permute-start(f32[2,3,128,128]{3,2,1,0:T(8,128)S(1)} %get-tuple-element.36), channel_id=1, source_target_pairs={{0,1},{1,2},{2,3},{3,4},{4,5},{5,6},{6,7},{7,8},{8,9},{9,10},{10,1... | collective-permute-start | bytes 1179656 | tf_op jit(solution)/shard_map/ppermute | solution.py:20
  46.1 1.3 collective-permute-start.6
  47.4 28.7 %all_to_all.31.parts = f32[16,8,128]{2,1,0:T(8,128)S(1)} all-to-all(f32[16,8,128]{2,1,0:T(8,128)S(1)} %fold_plane.2.after), channel_id=1, replica_groups={{0,32,64,96,128,160,192,224,256,288,320,352,384,416,448,480},{16,48,80,..., dimensions={0} | all-to-all | bytes 131072 | tf_op jit(solution)/shard_map/all_to_all | solution.py:37
  76.2 17.0 %all_to_all.32 = f32[32,8,128]{2,1,0:T(8,128)S(1)} all-to-all(f32[32,8,128]{2,1,0:T(8,128)S(1)} %fold_line.2), channel_id=1, replica_groups={{0,1,2,3,4,5,6,7,8,9,10,11,12,13,14,15,16,17,18,19,20,21,22,23,24,25,26..., dimensions={0} | all-to-all | bytes 262144 | tf_op jit(solution)/shard_map/all_to_all | solution.py:37
  93.2 6.2 %second_pass.1 = (f32[2,512,256]{2,1,0:T(8,128)}, f32[2,512,128]{2,1,0:T(8,128)}, f32[2,128,128]{2,1,0:T(8,128)}, f32[2,128,128]{2,1,0:T(8,128)}, f32[2,512,128]...) custom-call(s32[2,8]{1,0:T(2,128)S(1)} %bitcast.15, s32[1]{0:T(128)} %bitcast.10.counts, ...), custom_call_target="tpu_custom_call" | custom-call | tf_op jit(solution)/shard_map/second_pass/pallas_call | solution.py:327
  99.4 3.0 %collective-permute-start.7 = (f32[2,512,128]{2,1,0:T(8,128)}, f32[2,512,128]{2,1,0:T(8,128)S(1)}, u32[]{:S(2)}, u32[]{:S(2)}) collective-permute-start(f32[2,512,128]{2,1,0:T(8,128)} %get-tuple-element.42), channel_id=1, source_target_pairs={{0,16},{16,32},{32,48},{48,64},{64,80},{80,96},{96,112},{112,128},... | collective-permute-start | bytes 1572872 | tf_op jit(solution)/shard_map/ppermute | solution.py:24
  102.4 12.9 %all_to_all.33.parts = f32[32,8,128]{2,1,0:T(8,128)S(1)} all-to-all(f32[32,8,128]{2,1,0:T(8,128)} %bitcast.17), channel_id=1, replica_groups={{0,1,2,3,4,5,6,7,8,9,10,11,12,13,14,15,16,17,18,19,20,21,22,23,24,25,26..., dimensions={0} | all-to-all | bytes 262144 | tf_op jit(solution)/shard_map/all_to_all | solution.py:37
  116.0 3.9 %all-to-all-start.4 = ((f32[16,8,128]{2,1,0:T(8,128)}), f32[16,8,128]{2,1,0:T(8,128)S(1)}, u32[]{:S(2)}, u32[]{:S(2)}) async-start(f32[16,8,128]{2,1,0:T(8,128)} %fold_plane.3), calls=%async_computation.4 | async-start | bytes 131072 | tf_op jit(solution)/shard_map/all_to_all | solution.py:37
  119.9 2.0 %collective-permute-start.8 = (f32[2,2,128,128]{3,2,1,0:T(8,128)}, f32[2,2,128,128]{3,2,1,0:T(8,128)S(1)}, u32[]{:S(2)}, u32[]{:S(2)}) collective-permute-start(f32[2,2,128,128]{3,2,1,0:T(8,128)} %get-tuple-element.43), channel_id=1, source_target_pairs={{0,1},{1,2},{2,3},{3,4},{4,5},{5,6},{6,7},{7,8},{8,9},{9,10},{10,1... | collective-permute-start | bytes 786440 | tf_op jit(solution)/shard_map/ppermute | solution.py:20
  122.0 4.9 %collective-permute-start.9 = (f32[2,128,128]{2,1,0:T(8,128)}, f32[2,128,128]{2,1,0:T(8,128)S(1)}, u32[]{:S(2)}, u32[]{:S(2)}) collective-permute-start(f32[2,128,128]{2,1,0:T(8,128)} %get-tuple-element.44), channel_id=1, source_target_pairs={{0,17},{16,33},{32,49},{48,65},{64,81},{80,97},{96,113},{112,129},... | collective-permute-start | bytes 393224 | tf_op jit(solution)/shard_map/ppermute | solution.py:33
  126.8 4.8 %all-to-all-done.4.parts = f32[16,8,128]{2,1,0:T(8,128)S(1)} async-done(((f32[16,8,128]{2,1,0:T(8,128)}), f32[16,8,128]{2,1,0:T(8,128)S(1)}, u32[]{:S(2)}, u32[]{:S(2)}) %all-to-all-start.4) | async-done | bytes 65568 | tf_op jit(solution)/shard_map/all_to_all | solution.py:37
  132.4 5.5 %all-to-all-start.5 = ((f32[32,8,128]{2,1,0:T(8,128)}), f32[32,8,128]{2,1,0:T(8,128)S(1)}, u32[]{:S(2)}, u32[]{:S(2)}) async-start(f32[32,8,128]{2,1,0:T(8,128)} %fold_line.3), calls=%async_computation.5 | async-start | bytes 262144 | tf_op jit(solution)/shard_map/all_to_all | solution.py:37
  138.0 7.5 %all-to-all-done.5 = f32[32,8,128]{2,1,0:T(8,128)S(1)} async-done(((f32[32,8,128]{2,1,0:T(8,128)}), f32[32,8,128]{2,1,0:T(8,128)S(1)}, u32[]{:S(2)}, u32[]{:S(2)}) %all-to-all-start.5) | async-done | bytes 131104 | tf_op jit(solution)/shard_map/all_to_all | solution.py:37
  145.5 2.1 %finish.1 = (f32[2,512,256]{2,1,0:T(8,128)}, f32[2,128,128]{2,1,0:T(8,128)}) custom-call(f32[2,512,256]{2,1,0:T(8,128)} %get-tuple-element.39.obj_in, f32[2,512,128]{2,1,0:T(8,128)} %get-tuple-element.40.side_in, f32[2,128,128]{2,1,0:T(8,128)} %get-tuple-element.41.probe_in, ...), custom_call_target="tpu_custom_call", output_to_operand_aliasing={{0}: (0, {})} | custom-call | tf_op jit(solution)/shard_map/finish/pallas_call | solution.py:327
  (16 shorter events, 2.7 us)
Async XLA Ops:
  0.6 21.3 %copy-start = (s32[1,1,8,2]{2,3,1,0:T(2,128)S(1)}, s32[1,1,8,2]{2,3,1,0:T(2,128)}, u32[]{:S(2)}) copy-start(s32[1,1,8,2]{2,3,1,0:T(2,128)} %param.8) | copy-start | bytes 196
  1.8 20.1 %collective-permute-start.1 = (f32[2,512,128]{2,1,0:T(8,128)S(1)}, f32[2,512,128]{2,1,0:T(8,128)S(1)}, u32[]{:S(2)}, u32[]{:S(2)}) collective-permute-start(f32[2,512,128]{2,1,0:T(8,128)S(1)} %get-tuple-element.26), channel_id=1, source_target_pairs={{16,0},{32,16},{48,32},{64,48},{80,64},{96,80},{112,96},{128,112},... | collective-permute-start | bytes 1572872 | tf_op jit(solution)/shard_map/ppermute | solution.py:24
  10.6 11.3 %collective-permute-start = (f32[2,128,256]{2,1,0:T(8,128)S(1)}, f32[2,128,256]{2,1,0:T(8,128)S(1)}, u32[]{:S(2)}, u32[]{:S(2)}) collective-permute-start(f32[2,128,256]{2,1,0:T(8,128)S(1)} %get-tuple-element.25), channel_id=1, source_target_pairs={{1,0},{2,1},{3,2},{4,3},{5,4},{6,5},{7,6},{8,7},{9,8},{10,9},{11,1... | collective-permute-start | bytes 786440 | tf_op jit(solution)/shard_map/ppermute | solution.py:20
  11.9 7.3 %collective-permute-start.2 = (f32[2,128,128]{2,1,0:T(8,128)S(1)}, f32[2,128,128]{2,1,0:T(8,128)S(1)}, u32[]{:S(2)}, u32[]{:S(2)}) collective-permute-start(f32[2,128,128]{2,1,0:T(8,128)S(1)} %get-tuple-element.27), channel_id=1, source_target_pairs={{17,0},{33,16},{49,32},{65,48},{81,64},{97,80},{113,96},{129,112},... | collective-permute-start | bytes 393224 | tf_op jit(solution)/shard_map/ppermute | solution.py:33
  25.8 18.2 %collective-permute-start.4 = (f32[2,640,128]{2,1,0:T(8,128)S(1)}, f32[2,640,128]{2,1,0:T(8,128)S(1)}, u32[]{:S(2)}, u32[]{:S(2)}) collective-permute-start(f32[2,640,128]{2,1,0:T(8,128)S(1)} %get-tuple-element.32.acc_0), channel_id=1, source_target_pairs={{16,0},{32,16},{48,32},{64,48},{80,64},{96,80},{112,96},{128,112},... | collective-permute-start | bytes 1966088 | tf_op jit(solution)/shard_map/ppermute | solution.py:24
  28.2 15.7 %collective-permute-start.3 = (f32[2,640,128]{2,1,0:T(8,128)S(1)}, f32[2,640,128]{2,1,0:T(8,128)S(1)}, u32[]{:S(2)}, u32[]{:S(2)}) collective-permute-start(f32[2,640,128]{2,1,0:T(8,128)S(1)} %get-tuple-element.34.acc_2), channel_id=1, source_target_pairs={{0,16},{16,32},{32,48},{48,64},{64,80},{80,96},{96,112},{112,128},... | collective-permute-start | bytes 1966088 | tf_op jit(solution)/shard_map/ppermute | solution.py:24
  44.0 49.2 %collective-permute-start.5 = (f32[2,3,128,128]{3,2,1,0:T(8,128)S(1)}, f32[2,3,128,128]{3,2,1,0:T(8,128)S(1)}, u32[]{:S(2)}, u32[]{:S(2)}) collective-permute-start(f32[2,3,128,128]{3,2,1,0:T(8,128)S(1)} %get-tuple-element.36), channel_id=1, source_target_pairs={{0,1},{1,2},{2,3},{3,4},{4,5},{5,6},{6,7},{7,8},{8,9},{9,10},{10,1... | collective-permute-start | bytes 1179656 | tf_op jit(solution)/shard_map/ppermute | solution.py:20
  46.1 47.1 %collective-permute-start.6 = (f32[2,3,128,128]{3,2,1,0:T(8,128)S(1)}, f32[2,3,128,128]{3,2,1,0:T(8,128)S(1)}, u32[]{:S(2)}, u32[]{:S(2)}) collective-permute-start(f32[2,3,128,128]{3,2,1,0:T(8,128)S(1)} %get-tuple-element.37), channel_id=1, source_target_pairs={{1,0},{2,1},{3,2},{4,3},{5,4},{6,5},{7,6},{8,7},{9,8},{10,9},{11,1... | collective-permute-start | bytes 1179656 | tf_op jit(solution)/shard_map/ppermute | solution.py:20
  99.4 46.1 %collective-permute-start.7 = (f32[2,512,128]{2,1,0:T(8,128)}, f32[2,512,128]{2,1,0:T(8,128)S(1)}, u32[]{:S(2)}, u32[]{:S(2)}) collective-permute-start(f32[2,512,128]{2,1,0:T(8,128)} %get-tuple-element.42), channel_id=1, source_target_pairs={{0,16},{16,32},{32,48},{48,64},{64,80},{80,96},{96,112},{112,128},... | collective-permute-start | bytes 1572872 | tf_op jit(solution)/shard_map/ppermute | solution.py:24
  116.0 15.7 %all-to-all-start.4 = ((f32[16,8,128]{2,1,0:T(8,128)}), f32[16,8,128]{2,1,0:T(8,128)S(1)}, u32[]{:S(2)}, u32[]{:S(2)}) async-start(f32[16,8,128]{2,1,0:T(8,128)} %fold_plane.3), calls=%async_computation.4 | async-start | bytes 131072 | tf_op jit(solution)/shard_map/all_to_all | solution.py:37
  119.9 18.0 %collective-permute-start.8 = (f32[2,2,128,128]{3,2,1,0:T(8,128)}, f32[2,2,128,128]{3,2,1,0:T(8,128)S(1)}, u32[]{:S(2)}, u32[]{:S(2)}) collective-permute-start(f32[2,2,128,128]{3,2,1,0:T(8,128)} %get-tuple-element.43), channel_id=1, source_target_pairs={{0,1},{1,2},{2,3},{3,4},{4,5},{5,6},{6,7},{7,8},{8,9},{9,10},{10,1... | collective-permute-start | bytes 786440 | tf_op jit(solution)/shard_map/ppermute | solution.py:20
  122.0 16.0 %collective-permute-start.9 = (f32[2,128,128]{2,1,0:T(8,128)}, f32[2,128,128]{2,1,0:T(8,128)S(1)}, u32[]{:S(2)}, u32[]{:S(2)}) collective-permute-start(f32[2,128,128]{2,1,0:T(8,128)} %get-tuple-element.44), channel_id=1, source_target_pairs={{0,17},{16,33},{32,49},{48,65},{64,81},{80,97},{96,113},{112,129},... | collective-permute-start | bytes 393224 | tf_op jit(solution)/shard_map/ppermute | solution.py:33
  132.4 13.1 %all-to-all-start.5 = ((f32[32,8,128]{2,1,0:T(8,128)}), f32[32,8,128]{2,1,0:T(8,128)S(1)}, u32[]{:S(2)}, u32[]{:S(2)}) async-start(f32[32,8,128]{2,1,0:T(8,128)} %fold_line.3), calls=%async_computation.5 | async-start | bytes 262144 | tf_op jit(solution)/shard_map/all_to_all | solution.py:37

commit v4 on v3

--- a/solution.py
+++ b/solution.py
@@ -52,19 +52,25 @@
     return fold(swap(parts, ("tx", "ty"), plane), len(line[0]), "fold_plane")
 
 
-def sum_along(parts):
+def sum_along(parts, *after):
     plane, line = device_groups()
-    parts = fold(swap(parts, "tx", line), len(plane[0]), "fold_line")
-    parts = swap(parts, ("tx", "ty"), plane)
+    return fold(swap(parts, "tx", line), len(plane[0]), "fold_line", *after)
+
+
+def collect(parts):
+    parts = swap(parts, ("tx", "ty"), device_groups()[0])
     return parts.reshape(2, -1, parts.shape[-1])
 
 
-def fold(parts, copies, name):
-    (out,) = call(fold_kernel, name, (), (), [(copies, *parts.shape[1:])], [], 1, 1)(parts)
+def fold(parts, copies, name, *after):
+    (out,) = call(fold_kernel, name, (), (), [(copies, *parts.shape[1:])], [], 1, 2, (1,))(
+        parts, *after
+    )
     return out
 
 
-def fold_kernel(parts, out, sems):
+def fold_kernel(parts, *refs):
+    out = refs[-2]
     mine = parts[0]
     for at in range(1, parts.shape[0]):
         mine += parts[at]
@@ -233,8 +239,10 @@
             part[p] = acc[p, j]
 
 
-def strips_kernel(acc_0, acc_1, acc_2, from_left, from_right, after, up, down, sems):
-    del after
+def strips_kernel(
+    acc_0, acc_1, acc_2, from_left, from_right, after, own, up, down, sems
+):
+    del after, own
     width = up.shape[2]
     bottom = acc_0.shape[1] - width
     for p in range(2):
@@ -244,32 +252,48 @@
             block[p, 2] = acc_2[p, rows] + from_right[p, rows]
 
 
+def own_kernel(ext, acc_0, acc_1, acc_2, probe, cur, sems):
+    scale = peak_of(probe[0], probe[1])
+    for p in range(2):
+        for j, part in enumerate((acc_0, acc_1, acc_2)):
+            cur[p, j] = ext[p, j] - scale * part[p]
+
+
+def sides_kernel(old, from_left, from_right, probe, after, cur, sems):
+    del after
+    scale = peak_of(probe[0], probe[1])
+    last = cur.shape[1] - 1
+    for p in range(2):
+        cur[p, 0] = old[p, 0] - scale * from_left[p]
+        for j in range(1, last):
+            cur[p, j] = old[p, j]
+        cur[p, last] = old[p, last] - scale * from_right[p]
+
+
+def rims_kernel(old, from_up, from_down, probe, after, cur, sems):
+    del after
+    scale = peak_of(probe[0], probe[1])
+    width = cur.shape[3]
+    bottom = cur.shape[2] - width
+    for p in range(2):
+        for j in range(cur.shape[1]):
+            cur[p, j, :width] = old[p, j, :width] - scale * from_up[p, j]
+            cur[p, j, width:bottom] = old[p, j, width:bottom]
+            cur[p, j, bottom:] = old[p, j, bottom:] - scale * from_down[p, j]
+
+
 def second_kernel(
-    org, counts, ext, acc_0, acc_1, acc_2, from_left, from_right, from_up, from_down,
-    probe_in, gathered, share, inten_in, table_in,
+    org, counts, cur, probe_in, gathered, share, inten_in, table_in,
     obj_out, side_out, probe_out, total_out, right_out, down_out, corner_out,
-    cur, acc, own, probe, total, inten, table, sems,
+    acc, own, probe, total, inten, table, sems,
 ):
     n = cur.shape[1] - 1
     width = cur.shape[3]
     bottom = cur.shape[2] - width
     copies = Copies(sems)
     loads = copies.start((inten_in, inten), (table_in, table))
-    scale = peak_of(probe_in[0], probe_in[1])
-    mid = slice(width, bottom)
     for p in range(2):
         probe[p] = probe_in[p] - share[0] * gathered[p]
-        rows = ((slice(0, width), from_up), (mid, None), (slice(bottom, None), from_down))
-        for j, (part, side) in enumerate(
-            ((acc_0, from_left), (acc_1, None), (acc_2, from_right))
-        ):
-            for where, edge in rows:
-                value = part[p, where]
-                if side is not None:
-                    value += side[p, where]
-                if edge is not None:
-                    value += edge[p, j]
-                cur[p, j, where] = ext[p, j, where] - scale * value
     acc[...] = jnp.zeros_like(acc)
     total[...] = jnp.zeros_like(total)
     wait(loads)
@@ -314,14 +338,15 @@
     wait(stores)
 
 
-def call(kernel, name, smem, far, outs, scratch, copies, mib, **more):
+def call(kernel, name, smem, far, outs, scratch, copies, mib, unread=(), **more):
     kinds = {True: pltpu.HBM, False: pltpu.VMEM}
 
     def run(*operands):
         where = [pltpu.SMEM if at in smem else kinds[at in far] for at in range(len(operands))]
         held = [kinds[-1 - at in far] for at in range(len(outs))]
+        where = [pl.ANY if at in unread else space for at, space in enumerate(where)]
         operands = [
-            value if space is pltpu.SMEM else pltpu.with_memory_space_constraint(value, space)
+            value if space in (pltpu.SMEM, pl.ANY) else pltpu.with_memory_space_constraint(value, space)
             for value, space in zip(operands, where)
         ]
         return pl.pallas_call(
@@ -364,26 +389,34 @@
         [blocks, square, slots, kept, slots], [slots], 6, 4,
     )(object_planes, probe, inten, table)
     ext, acc_0, acc_1, acc_2, total = call(
-        first_kernel, "first_pass", (0, 1), (), [blocks, tall, tall, tall, square], [blocks], 1, 6
+        first_kernel, "first_pass", (0, 1), (), [blocks, tall, tall, tall, square], [blocks], 1, 8
     )(org, count, ext, below, right, corner, start, inten_near, table_near)
     from_left, from_right = shift(acc_2, 0, 1), shift(acc_0, 0, -1)
+    hint = pl.CostEstimate(flops=1 << 20, bytes_accessed=1 << 23, transcendentals=0)
+    (cur,) = call(own_kernel, "own_step", (), (), [blocks], [], 1, 8, cost_estimate=hint)(
+        ext, acc_0, acc_1, acc_2, start
+    )
     parts = sum_in_plane(total)
-    up, down = call(strips_kernel, "strips", (), (), [strip, strip], [], 1, 1)(
-        acc_0, acc_1, acc_2, from_left, from_right, parts
+    up, down = call(strips_kernel, "strips", (), (), [strip, strip], [], 1, 6, (5, 6))(
+        acc_0, acc_1, acc_2, from_left, from_right, parts, cur
     )
     from_up, from_down = shift(down, 1, 0), shift(up, -1, 0)
-    gathered = sum_along(parts)
+    (cur,) = call(sides_kernel, "sides_step", (), (), [blocks], [], 1, 8, (4,), cost_estimate=hint)(
+        cur, from_left, from_right, start, parts
+    )
+    parts = sum_along(parts, cur)
+    (cur,) = call(rims_kernel, "rims_step", (), (), [blocks], [], 1, 8, (4,), cost_estimate=hint)(
+        cur, from_up, from_down, start, parts
+    )
+    gathered = collect(parts)
     obj, side, current, total, to_right, to_down, to_corner = call(
-        second_kernel, "second_pass", (0, 1, 12), (13, 14, *range(-7, 0)),
+        second_kernel, "second_pass", (0, 1, 5), (6, 7, *range(-7, 0)),
         [(2, rows, cols), (2, rows, w), square, square, (2, rows, w), (2, n, w, w), square],
-        [blocks, blocks, (2, n, rows, w), square, square, slots, kept], n + 7, 9,
-    )(
-        org, count, ext, acc_0, acc_1, acc_2, from_left, from_right, from_up, from_down,
-        start, gathered, share, inten, table,
-    )
+        [blocks, (2, n, rows, w), square, square, slots, kept], n + 7, 10,
+    )(org, count, cur, start, gathered, share, inten, table)
     from_left, from_up = shift(to_right, 0, 1), shift(to_down, 1, 0)
     from_corner = shift(to_corner, 1, 1)
-    gathered = sum_along(sum_in_plane(total))
+    gathered = collect(sum_along(sum_in_plane(total)))
     obj, current = call(
         final_kernel, "finish", (7,), (0, 1, 2, -1, -2), [(2, rows, cols), square],
         [(2, rows, w), (2, n - 1, w, w), square], 2 * n + 2, 3, input_output_aliases={0: 0},

time: 148 us -> 156 us (1.054)
  blocking collectives: 71.2 us -> 10.6 us
  starting transfers between devices: 39.6 us -> 76.2 us
  waiting for transfers between devices: 18.3 us -> 37.3 us
  local copies, waits for them, and re-layouts: 0.01 us -> 7.19 us
  Pallas kernels: 16.9 us -> 21.7 us
    all_to_all x4 -> x1, blocking collectives: 71.2 us -> 10.6 us  [swap(): lax.all_to_all(parts, axes, 0, 0, axis_index_groups=groups, tiled=True)]
    all_to_all x2 -> x5, starting transfers between devices: 9.47 us -> 41.6 us  [swap(): lax.all_to_all(parts, axes, 0, 0, axis_index_groups=groups, tiled=True)]
    all_to_all x2 -> x5, waiting for transfers between devices: 12.4 us -> 31.3 us  [swap(): lax.all_to_all(parts, axes, 0, 0, axis_index_groups=groups, tiled=True)]
    unnamed x2 -> x14, local copies, waits for them, and re-layouts: 0.01 us -> 7.19 us
    pallas_call x10 -> x13, Pallas kernels: 16.9 us -> 21.7 us  [run(): pl.pallas_call(kernel, out_shape=[space(s, F32) if isinstance(s, tuple) e...]
    ppermute x4, starting transfers between devices: 17.3 us -> 21.8 us  [shift(): lax.ppermute(value, 'tx', [(b, b + cols) for b in range(n_c) if 0 <= b +...]
  transfers between devices with their start and end apart: 12 -> 15, of which waited for: 4 -> 7; matrix products, arithmetic and copies ran while one was open for 0% -> 0% of each run, Pallas kernels for 2% -> 5%
where the time goes in v4:
time: 156 us; the launch traced here: 155 us
  starting transfers between devices  76.2 us (49%)
  waiting for transfers between devices  37.3 us (24%)
  Pallas kernels  21.7 us (14%)
  blocking collectives  10.6 us (7%)
  local copies, waits for them, and re-layouts  7.19 us (5%)
  between operations  1.6 us (1%)
    all_to_all x5, starting transfers between devices, swap(): lax.all_to_all(parts, axes, 0, 0, axis_index_groups=groups, tiled=True)  41.6 us
    all_to_all x5, waiting for transfers between devices, swap(): lax.all_to_all(parts, axes, 0, 0, axis_index_groups=groups, tiled=True)  31.3 us
    ppermute x4, starting transfers between devices, shift(): lax.ppermute(value, 'tx', [(b, b + cols) for b in range(n_c) if 0 <= b +...  21.8 us
    pallas_call x13, Pallas kernels, run(): pl.pallas_call(kernel, out_shape=[space(s, F32) if isinstance(s, tuple) e...  21.7 us
    all_to_all x1, blocking collectives, swap(): lax.all_to_all(parts, axes, 0, 0, axis_index_groups=groups, tiled=True)  10.6 us
    unnamed x14, local copies, waits for them, and re-layouts  7.19 us
    ppermute x4, starting transfers between devices, shift(): lax.ppermute(value, 'ty', [(a, a + rows) for a in range(n_r) if 0 <= a +...  6.66 us
    ppermute x2, starting transfers between devices, shift(): return lax.ppermute(value, ('tx', 'ty'), pairs)  6.14 us
  transfers between devices with their start and end apart: 15, of which 7 were waited for; matrix products, arithmetic and copies ran while one was open for 0% of the time, Pallas kernels for 5%

profile of v4, /device:TPU:1, one launch (start us, length us, event | category | flops | bytes accessed | tf_op | source)
XLA Modules:
  0.0 154.7 jit_solution(4722045235772001307)
XLA Ops:
  1.8 8.8 %collective-permute-start.1 = (f32[2,512,128]{2,1,0:T(8,128)S(1)}, f32[2,512,128]{2,1,0:T(8,128)S(1)}, u32[]{:S(2)}, u32[]{:S(2)}) collective-permute-start(f32[2,512,128]{2,1,0:T(8,128)S(1)} %get-tuple-element.26), channel_id=1, source_target_pairs={{16,0},{32,16},{48,32},{64,48},{80,64},{96,80},{112,96},{128,112},... | collective-permute-start | bytes 1572872 | tf_op jit(solution)/shard_map/ppermute | solution.py:24
  13.9 2.1 %prepare.1 = (f32[2,3,640,128]{3,2,1,0:T(8,128)S(1)}, f32[2,128,128]{2,1,0:T(8,128)S(1)}, f32[8,128,128]{2,1,0:T(8,128)S(1)}, bf16[768,256]{1,0:T(8,128)(2,1)S(1)}, f32[8,128,128]{2,1,0:T(8,128)}) custom-call(f32[2,512,256]{2,1,0:T(8,128)} %tile.3, f32[2,128,128]{2,1,0:T(8,128)} %probe_in.1, f32[8,128,128]{2,1,0:T(8,128)} %bitcast.15, ...), custom_call_target="tpu_custom_call" | custom-call | tf_op jit(solution)/shard_map/prepare/pallas_call | solution.py:352
  16.0 3.3 %collective-permute-done.2.corner = f32[2,128,128]{2,1,0:T(8,128)S(1)} collective-permute-done((f32[2,128,128]{2,1,0:T(8,128)S(1)}, f32[2,128,128]{2,1,0:T(8,128)S(1)}, u32[]{:S(2)}, u32[]{:S(2)}) %collective-permute-start.2) | collective-permute-done | bytes 131104 | tf_op jit(solution)/shard_map/ppermute | solution.py:33
  19.2 2.7 %collective-permute-done.below = f32[2,128,256]{2,1,0:T(8,128)S(1)} collective-permute-done((f32[2,128,256]{2,1,0:T(8,128)S(1)}, f32[2,128,256]{2,1,0:T(8,128)S(1)}, u32[]{:S(2)}, u32[]{:S(2)}) %collective-permute-start) | collective-permute-done | bytes 262176 | tf_op jit(solution)/shard_map/ppermute | solution.py:20
  22.0 3.1 %first_pass.1 = (f32[2,3,640,128]{3,2,1,0:T(8,128)S(1)}, f32[2,640,128]{2,1,0:T(8,128)S(1)}, f32[2,640,128]{2,1,0:T(8,128)S(1)}, f32[2,640,128]{2,1,0:T(8,128)}, f32[2,128,128]{2,1,0:T(8,128)}) custom-call(s32[2,8]{1,0:T(2,128)S(1)} %bitcast.13, s32[1]{0:T(128)} %bitcast.9.counts, f32[2,3,640,128]{3,2,1,0:T(8,128)S(1)} %get-tuple-element.24.ext_in, ...), custom_call_target="tpu_custom_call" | custom-call | tf_op jit(solution)/shard_map/first_pass/pallas_call | solution.py:352
  26.4 5.3 %collective-permute-start.4 = (f32[2,640,128]{2,1,0:T(8,128)S(1)}, f32[2,640,128]{2,1,0:T(8,128)}, u32[]{:S(2)}, u32[]{:S(2)}) collective-permute-start(f32[2,640,128]{2,1,0:T(8,128)S(1)} %get-tuple-element.32.acc_0), channel_id=1, source_target_pairs={{16,0},{32,16},{48,32},{64,48},{80,64},{96,80},{112,96},{128,112},... | collective-permute-start | bytes 1966088 | tf_op jit(solution)/shard_map/ppermute | solution.py:24
  33.6 6.4 %all-to-all-start = ((f32[32,8,128]{2,1,0:T(8,128)}), f32[32,8,128]{2,1,0:T(8,128)S(1)}, u32[]{:S(2)}, u32[]{:S(2)}) async-start(f32[32,8,128]{2,1,0:T(8,128)} %bitcast.5), calls=%async_computation | async-start | bytes 262144 | tf_op jit(solution)/shard_map/all_to_all | solution.py:37
  43.1 4.5 %all-to-all-done.parts = f32[32,8,128]{2,1,0:T(8,128)S(1)} async-done(((f32[32,8,128]{2,1,0:T(8,128)}), f32[32,8,128]{2,1,0:T(8,128)S(1)}, u32[]{:S(2)}, u32[]{:S(2)}) %all-to-all-start) | async-done | bytes 131104 | tf_op jit(solution)/shard_map/all_to_all | solution.py:37
  48.3 2.4 %strips.1 = (f32[2,3,128,128]{3,2,1,0:T(8,128)}, f32[2,3,128,128]{3,2,1,0:T(8,128)}) custom-call(f32[2,640,128]{2,1,0:T(8,128)S(1)} %get-tuple-element.32.acc_0, f32[2,640,128]{2,1,0:T(8,128)S(1)} %get-tuple-element.33.acc_1, f32[2,640,128]{2,1,0:T(8,128)} %get-tuple-element.34.acc_2, f32[2,640,128]{2,1,0:T(8,128)} %collective-permute-done.3.from_left, ...), custom_call_target="tpu_custom_call" | custom-call | tf_op jit(solution)/shard_map/strips/pallas_call | solution.py:352
  50.8 2.0 %collective-permute-start.5 = (f32[2,3,128,128]{3,2,1,0:T(8,128)}, f32[2,3,128,128]{3,2,1,0:T(8,128)S(1)}, u32[]{:S(2)}, u32[]{:S(2)}) collective-permute-start(f32[2,3,128,128]{3,2,1,0:T(8,128)} %get-tuple-element.36), channel_id=1, source_target_pairs={{0,1},{1,2},{2,3},{3,4},{4,5},{5,6},{6,7},{7,8},{8,9},{9,10},{10,1... | collective-permute-start | bytes 1179656 | tf_op jit(solution)/shard_map/ppermute | solution.py:20
  54.1 14.5 %all-to-all-start.1 = ((f32[16,8,128]{2,1,0:T(8,128)}), f32[16,8,128]{2,1,0:T(8,128)S(1)}, u32[]{:S(2)}, u32[]{:S(2)}) async-start(f32[16,8,128]{2,1,0:T(8,128)} %fold_plane.2.after), calls=%async_computation.1 | async-start | bytes 131072 | tf_op jit(solution)/shard_map/all_to_all | solution.py:37
  71.7 8.4 %all-to-all-done.1.parts = f32[16,8,128]{2,1,0:T(8,128)S(1)} async-done(((f32[16,8,128]{2,1,0:T(8,128)}), f32[16,8,128]{2,1,0:T(8,128)S(1)}, u32[]{:S(2)}, u32[]{:S(2)}) %all-to-all-start.1) | async-done | bytes 65568 | tf_op jit(solution)/shard_map/all_to_all | solution.py:37
  80.9 9.7 %all-to-all-start.2 = ((f32[32,8,128]{2,1,0:T(8,128)}), f32[32,8,128]{2,1,0:T(8,128)S(1)}, u32[]{:S(2)}, u32[]{:S(2)}) async-start(f32[32,8,128]{2,1,0:T(8,128)} %fold_line.2.after), calls=%async_computation.2 | async-start | bytes 262144 | tf_op jit(solution)/shard_map/all_to_all | solution.py:37
  92.1 6.0 %all-to-all-done.2 = f32[32,8,128]{2,1,0:T(8,128)S(1)} async-done(((f32[32,8,128]{2,1,0:T(8,128)}), f32[32,8,128]{2,1,0:T(8,128)S(1)}, u32[]{:S(2)}, u32[]{:S(2)}) %all-to-all-start.2) | async-done | bytes 131104 | tf_op jit(solution)/shard_map/all_to_all | solution.py:37
  99.7 4.8 %second_pass.1 = (f32[2,512,256]{2,1,0:T(8,128)}, f32[2,512,128]{2,1,0:T(8,128)}, f32[2,128,128]{2,1,0:T(8,128)}, f32[2,128,128]{2,1,0:T(8,128)}, f32[2,512,128]...) custom-call(s32[2,8]{1,0:T(2,128)S(1)} %bitcast.14, s32[1]{0:T(128)} %bitcast.10.counts, ...), custom_call_target="tpu_custom_call" | custom-call | tf_op jit(solution)/shard_map/second_pass/pallas_call | solution.py:352
  104.5 5.8 %collective-permute-start.7 = (f32[2,512,128]{2,1,0:T(8,128)}, f32[2,512,128]{2,1,0:T(8,128)S(1)}, u32[]{:S(2)}, u32[]{:S(2)}) collective-permute-start(f32[2,512,128]{2,1,0:T(8,128)} %get-tuple-element.42), channel_id=1, source_target_pairs={{0,16},{16,32},{32,48},{48,64},{64,80},{80,96},{96,112},{112,128},... | collective-permute-start | bytes 1572872 | tf_op jit(solution)/shard_map/ppermute | solution.py:24
  110.3 10.6 %all_to_all.30.parts = f32[32,8,128]{2,1,0:T(8,128)S(1)} all-to-all(f32[32,8,128]{2,1,0:T(8,128)} %bitcast.16), channel_id=1, replica_groups={{0,1,2,3,4,5,6,7,8,9,10,11,12,13,14,15,16,17,18,19,20,21,22,23,24,25,26..., dimensions={0} | all-to-all | bytes 262144 | tf_op jit(solution)/shard_map/all_to_all | solution.py:37
  121.6 5.4 %all-to-all-start.4 = ((f32[16,8,128]{2,1,0:T(8,128)}), f32[16,8,128]{2,1,0:T(8,128)S(1)}, u32[]{:S(2)}, u32[]{:S(2)}) async-start(f32[16,8,128]{2,1,0:T(8,128)} %fold_plane.3), calls=%async_computation.4 | async-start | bytes 131072 | tf_op jit(solution)/shard_map/all_to_all | solution.py:37
  127.1 2.0 %collective-permute-start.8 = (f32[2,2,128,128]{3,2,1,0:T(8,128)}, f32[2,2,128,128]{3,2,1,0:T(8,128)S(1)}, u32[]{:S(2)}, u32[]{:S(2)}) collective-permute-start(f32[2,2,128,128]{3,2,1,0:T(8,128)} %get-tuple-element.43), channel_id=1, source_target_pairs={{0,1},{1,2},{2,3},{3,4},{4,5},{5,6},{6,7},{7,8},{8,9},{9,10},{10,1... | collective-permute-start | bytes 786440 | tf_op jit(solution)/shard_map/ppermute | solution.py:20
  129.1 4.9 %collective-permute-start.9 = (f32[2,128,128]{2,1,0:T(8,128)}, f32[2,128,128]{2,1,0:T(8,128)S(1)}, u32[]{:S(2)}, u32[]{:S(2)}) collective-permute-start(f32[2,128,128]{2,1,0:T(8,128)} %get-tuple-element.44), channel_id=1, source_target_pairs={{0,17},{16,33},{32,49},{48,65},{64,81},{80,97},{96,113},{112,129},... | collective-permute-start | bytes 393224 | tf_op jit(solution)/shard_map/ppermute | solution.py:33
  134.0 4.8 %all-to-all-done.4.parts = f32[16,8,128]{2,1,0:T(8,128)S(1)} async-done(((f32[16,8,128]{2,1,0:T(8,128)}), f32[16,8,128]{2,1,0:T(8,128)S(1)}, u32[]{:S(2)}, u32[]{:S(2)}) %all-to-all-start.4) | async-done | bytes 65568 | tf_op jit(solution)/shard_map/all_to_all | solution.py:37
  139.5 5.5 %all-to-all-start.5 = ((f32[32,8,128]{2,1,0:T(8,128)}), f32[32,8,128]{2,1,0:T(8,128)S(1)}, u32[]{:S(2)}, u32[]{:S(2)}) async-start(f32[32,8,128]{2,1,0:T(8,128)} %fold_line.3), calls=%async_computation.5 | async-start | bytes 262144 | tf_op jit(solution)/shard_map/all_to_all | solution.py:37
  145.1 7.5 %all-to-all-done.5 = f32[32,8,128]{2,1,0:T(8,128)S(1)} async-done(((f32[32,8,128]{2,1,0:T(8,128)}), f32[32,8,128]{2,1,0:T(8,128)S(1)}, u32[]{:S(2)}, u32[]{:S(2)}) %all-to-all-start.5) | async-done | bytes 131104 | tf_op jit(solution)/shard_map/all_to_all | solution.py:37
  152.6 2.1 %finish.1 = (f32[2,512,256]{2,1,0:T(8,128)}, f32[2,128,128]{2,1,0:T(8,128)}) custom-call(f32[2,512,256]{2,1,0:T(8,128)} %get-tuple-element.39.obj_in, f32[2,512,128]{2,1,0:T(8,128)} %get-tuple-element.40.side_in, f32[2,128,128]{2,1,0:T(8,128)} %get-tuple-element.41.probe_in, ...), custom_call_target="tpu_custom_call", output_to_operand_aliasing={{0}: (0, {})} | custom-call | tf_op jit(solution)/shard_map/finish/pallas_call | solution.py:352
  (34 shorter events, 20.2 us)
Async XLA Ops:
  0.6 21.3 %copy-start.6 = (s32[1,1,8,2]{2,3,1,0:T(2,128)S(1)}, s32[1,1,8,2]{2,3,1,0:T(2,128)}, u32[]{:S(2)}) copy-start(s32[1,1,8,2]{2,3,1,0:T(2,128)} %param.8) | copy-start | bytes 196
  1.8 20.1 %collective-permute-start.1 = (f32[2,512,128]{2,1,0:T(8,128)S(1)}, f32[2,512,128]{2,1,0:T(8,128)S(1)}, u32[]{:S(2)}, u32[]{:S(2)}) collective-permute-start(f32[2,512,128]{2,1,0:T(8,128)S(1)} %get-tuple-element.26), channel_id=1, source_target_pairs={{16,0},{32,16},{48,32},{64,48},{80,64},{96,80},{112,96},{128,112},... | collective-permute-start | bytes 1572872 | tf_op jit(solution)/shard_map/ppermute | solution.py:24
  10.6 11.3 %collective-permute-start = (f32[2,128,256]{2,1,0:T(8,128)S(1)}, f32[2,128,256]{2,1,0:T(8,128)S(1)}, u32[]{:S(2)}, u32[]{:S(2)}) collective-permute-start(f32[2,128,256]{2,1,0:T(8,128)S(1)} %get-tuple-element.25), channel_id=1, source_target_pairs={{1,0},{2,1},{3,2},{4,3},{5,4},{6,5},{7,6},{8,7},{9,8},{10,9},{11,1... | collective-permute-start | bytes 786440 | tf_op jit(solution)/shard_map/ppermute | solution.py:20
  11.9 7.3 %collective-permute-start.2 = (f32[2,128,128]{2,1,0:T(8,128)S(1)}, f32[2,128,128]{2,1,0:T(8,128)S(1)}, u32[]{:S(2)}, u32[]{:S(2)}) collective-permute-start(f32[2,128,128]{2,1,0:T(8,128)S(1)} %get-tuple-element.27), channel_id=1, source_target_pairs={{17,0},{33,16},{49,32},{65,48},{81,64},{97,80},{113,96},{129,112},... | collective-permute-start | bytes 393224 | tf_op jit(solution)/shard_map/ppermute | solution.py:33
  25.1 1.3 copy-start.4
  26.4 21.9 %collective-permute-start.4 = (f32[2,640,128]{2,1,0:T(8,128)S(1)}, f32[2,640,128]{2,1,0:T(8,128)}, u32[]{:S(2)}, u32[]{:S(2)}) collective-permute-start(f32[2,640,128]{2,1,0:T(8,128)S(1)} %get-tuple-element.32.acc_0), channel_id=1, source_target_pairs={{16,0},{32,16},{48,32},{64,48},{80,64},{96,80},{112,96},{128,112},... | collective-permute-start | bytes 1966088 | tf_op jit(solution)/shard_map/ppermute | solution.py:24
  31.7 16.6 %collective-permute-start.3 = (f32[2,640,128]{2,1,0:T(8,128)}, f32[2,640,128]{2,1,0:T(8,128)}, u32[]{:S(2)}, u32[]{:S(2)}) collective-permute-start(f32[2,640,128]{2,1,0:T(8,128)} %get-tuple-element.34.acc_2), channel_id=1, source_target_pairs={{0,16},{16,32},{32,48},{48,64},{64,80},{80,96},{96,112},{112,128},... | collective-permute-start | bytes 1966088 | tf_op jit(solution)/shard_map/ppermute | solution.py:24
  33.6 14.0 %all-to-all-start = ((f32[32,8,128]{2,1,0:T(8,128)}), f32[32,8,128]{2,1,0:T(8,128)S(1)}, u32[]{:S(2)}, u32[]{:S(2)}) async-start(f32[32,8,128]{2,1,0:T(8,128)} %bitcast.5), calls=%async_computation | async-start | bytes 262144 | tf_op jit(solution)/shard_map/all_to_all | solution.py:37
  40.1 1.5 copy-start.5
  43.1 7.7 %copy-start = (f32[2,3,640,128]{3,2,1,0:T(8,128)}, f32[2,3,640,128]{3,2,1,0:T(8,128)S(1)}, u32[]{:S(2)}) copy-start(f32[2,3,640,128]{3,2,1,0:T(8,128)S(1)} %own_step.1.old.own) | copy-start | bytes 5898244
  50.8 39.8 %collective-permute-start.5 = (f32[2,3,128,128]{3,2,1,0:T(8,128)}, f32[2,3,128,128]{3,2,1,0:T(8,128)S(1)}, u32[]{:S(2)}, u32[]{:S(2)}) collective-permute-start(f32[2,3,128,128]{3,2,1,0:T(8,128)} %get-tuple-element.36), channel_id=1, source_target_pairs={{0,1},{1,2},{2,3},{3,4},{4,5},{5,6},{6,7},{7,8},{8,9},{9,10},{10,1... | collective-permute-start | bytes 1179656 | tf_op jit(solution)/shard_map/ppermute | solution.py:20
  52.8 37.8 %collective-permute-start.6 = (f32[2,3,128,128]{3,2,1,0:T(8,128)}, f32[2,3,128,128]{3,2,1,0:T(8,128)S(1)}, u32[]{:S(2)}, u32[]{:S(2)}) collective-permute-start(f32[2,3,128,128]{3,2,1,0:T(8,128)} %get-tuple-element.37), channel_id=1, source_target_pairs={{1,0},{2,1},{3,2},{4,3},{5,4},{6,5},{7,6},{8,7},{9,8},{10,9},{11,1... | collective-permute-start | bytes 1179656 | tf_op jit(solution)/shard_map/ppermute | solution.py:20
  54.1 26.1 %all-to-all-start.1 = ((f32[16,8,128]{2,1,0:T(8,128)}), f32[16,8,128]{2,1,0:T(8,128)S(1)}, u32[]{:S(2)}, u32[]{:S(2)}) async-start(f32[16,8,128]{2,1,0:T(8,128)} %fold_plane.2.after), calls=%async_computation.1 | async-start | bytes 131072 | tf_op jit(solution)/shard_map/all_to_all | solution.py:37
  68.6 1.5 copy-start.1
  80.9 17.2 %all-to-all-start.2 = ((f32[32,8,128]{2,1,0:T(8,128)}), f32[32,8,128]{2,1,0:T(8,128)S(1)}, u32[]{:S(2)}, u32[]{:S(2)}) async-start(f32[32,8,128]{2,1,0:T(8,128)} %fold_line.2.after), calls=%async_computation.2 | async-start | bytes 262144 | tf_op jit(solution)/shard_map/all_to_all | solution.py:37
  90.8 1.3 copy-start.2
  98.1 1.5 copy-start.3
  104.5 48.1 %collective-permute-start.7 = (f32[2,512,128]{2,1,0:T(8,128)}, f32[2,512,128]{2,1,0:T(8,128)S(1)}, u32[]{:S(2)}, u32[]{:S(2)}) collective-permute-start(f32[2,512,128]{2,1,0:T(8,128)} %get-tuple-element.42), channel_id=1, source_target_pairs={{0,16},{16,32},{32,48},{48,64},{64,80},{80,96},{96,112},{112,128},... | collective-permute-start | bytes 1572872 | tf_op jit(solution)/shard_map/ppermute | solution.py:24
  121.6 17.2 %all-to-all-start.4 = ((f32[16,8,128]{2,1,0:T(8,128)}), f32[16,8,128]{2,1,0:T(8,128)S(1)}, u32[]{:S(2)}, u32[]{:S(2)}) async-start(f32[16,8,128]{2,1,0:T(8,128)} %fold_plane.3), calls=%async_computation.4 | async-start | bytes 131072 | tf_op jit(solution)/shard_map/all_to_all | solution.py:37
  127.1 18.0 %collective-permute-start.8 = (f32[2,2,128,128]{3,2,1,0:T(8,128)}, f32[2,2,128,128]{3,2,1,0:T(8,128)S(1)}, u32[]{:S(2)}, u32[]{:S(2)}) collective-permute-start(f32[2,2,128,128]{3,2,1,0:T(8,128)} %get-tuple-element.43), channel_id=1, source_target_pairs={{0,1},{1,2},{2,3},{3,4},{4,5},{5,6},{6,7},{7,8},{8,9},{9,10},{10,1... | collective-permute-start | bytes 786440 | tf_op jit(solution)/shard_map/ppermute | solution.py:20
  129.1 16.0 %collective-permute-start.9 = (f32[2,128,128]{2,1,0:T(8,128)}, f32[2,128,128]{2,1,0:T(8,128)S(1)}, u32[]{:S(2)}, u32[]{:S(2)}) collective-permute-start(f32[2,128,128]{2,1,0:T(8,128)} %get-tuple-element.44), channel_id=1, source_target_pairs={{0,17},{16,33},{32,49},{48,65},{64,81},{80,97},{96,113},{112,129},... | collective-permute-start | bytes 393224 | tf_op jit(solution)/shard_map/ppermute | solution.py:33
  139.5 13.1 %all-to-all-start.5 = ((f32[32,8,128]{2,1,0:T(8,128)}), f32[32,8,128]{2,1,0:T(8,128)S(1)}, u32[]{:S(2)}, u32[]{:S(2)}) async-start(f32[32,8,128]{2,1,0:T(8,128)} %fold_line.3), calls=%async_computation.5 | async-start | bytes 262144 | tf_op jit(solution)/shard_map/all_to_all | solution.py:37

commit v5 on v3

--- a/solution.py
+++ b/solution.py
@@ -8,7 +8,7 @@
 
 step_object = 1.0
 step_probe = 1.0
-GROUP = 2
+GROUP = 4
 CORES = 2
 F32 = jnp.float32
 BF16 = jnp.bfloat16
@@ -364,7 +364,7 @@
         [blocks, square, slots, kept, slots], [slots], 6, 4,
     )(object_planes, probe, inten, table)
     ext, acc_0, acc_1, acc_2, total = call(
-        first_kernel, "first_pass", (0, 1), (), [blocks, tall, tall, tall, square], [blocks], 1, 6
+        first_kernel, "first_pass", (0, 1), (), [blocks, tall, tall, tall, square], [blocks], 1, 8
     )(org, count, ext, below, right, corner, start, inten_near, table_near)
     from_left, from_right = shift(acc_2, 0, 1), shift(acc_0, 0, -1)
     parts = sum_in_plane(total)
@@ -376,7 +376,7 @@
     obj, side, current, total, to_right, to_down, to_corner = call(
         second_kernel, "second_pass", (0, 1, 12), (13, 14, *range(-7, 0)),
         [(2, rows, cols), (2, rows, w), square, square, (2, rows, w), (2, n, w, w), square],
-        [blocks, blocks, (2, n, rows, w), square, square, slots, kept], n + 7, 9,
+        [blocks, blocks, (2, n, rows, w), square, square, slots, kept], n + 7, 11,
     )(
         org, count, ext, acc_0, acc_1, acc_2, from_left, from_right, from_up, from_down,
         start, gathered, share, inten, table,

time: 148 us -> 146 us (0.986)
  blocking collectives: 71.2 us -> 67.7 us
  starting transfers between devices: 39.6 us -> 42 us
  Pallas kernels: 16.9 us -> 15.4 us
    all_to_all x4, blocking collectives: 71.2 us -> 67.7 us  [swap(): lax.all_to_all(parts, axes, 0, 0, axis_index_groups=groups, tiled=True)]
    ppermute x4, starting transfers between devices: 17.3 us -> 19.7 us  [shift(): lax.ppermute(value, 'tx', [(b, b + cols) for b in range(n_c) if 0 <= b +...]
    pallas_call x10, Pallas kernels: 16.9 us -> 15.4 us  [run(): pl.pallas_call(kernel, out_shape=[space(s, F32) if isinstance(s, tuple) e...]
where the time goes in v5:
time: 146 us; the launch traced here: 145 us
  blocking collectives  67.7 us (46%)
  starting transfers between devices  42 us (29%)
  waiting for transfers between devices  18.3 us (13%)
  Pallas kernels  15.4 us (11%)
  between operations  1.49 us (1%)
    all_to_all x4, blocking collectives, swap(): lax.all_to_all(parts, axes, 0, 0, axis_index_groups=groups, tiled=True)  67.7 us
    ppermute x4, starting transfers between devices, shift(): lax.ppermute(value, 'tx', [(b, b + cols) for b in range(n_c) if 0 <= b +...  19.7 us
    pallas_call x10, Pallas kernels, run(): pl.pallas_call(kernel, out_shape=[space(s, F32) if isinstance(s, tuple) e...  15.4 us
    all_to_all x2, waiting for transfers between devices, swap(): lax.all_to_all(parts, axes, 0, 0, axis_index_groups=groups, tiled=True)  12.4 us
    all_to_all x2, starting transfers between devices, swap(): lax.all_to_all(parts, axes, 0, 0, axis_index_groups=groups, tiled=True)  9.54 us
    ppermute x4, starting transfers between devices, shift(): lax.ppermute(value, 'ty', [(a, a + rows) for a in range(n_r) if 0 <= a +...  6.66 us
    ppermute x2, starting transfers between devices, shift(): return lax.ppermute(value, ('tx', 'ty'), pairs)  6.14 us
    ppermute x2, waiting for transfers between devices, shift(): return lax.ppermute(value, ('tx', 'ty'), pairs)  3.24 us
  transfers between devices with their start and end apart: 12, of which 4 were waited for; matrix products, arithmetic and copies ran while one was open for 0% of the time, Pallas kernels for 2%

profile of v5, /device:TPU:1, one launch (start us, length us, event | category | flops | bytes accessed | tf_op | source)
XLA Modules:
  0.0 144.9 jit_solution(12456629500875979863)
XLA Ops:
  1.8 8.8 %collective-permute-start.1 = (f32[2,512,128]{2,1,0:T(8,128)S(1)}, f32[2,512,128]{2,1,0:T(8,128)S(1)}, u32[]{:S(2)}, u32[]{:S(2)}) collective-permute-start(f32[2,512,128]{2,1,0:T(8,128)S(1)} %get-tuple-element.26), channel_id=1, source_target_pairs={{16,0},{32,16},{48,32},{64,48},{80,64},{96,80},{112,96},{128,112},... | collective-permute-start | bytes 1572872 | tf_op jit(solution)/shard_map/ppermute | solution.py:24
  10.6 1.3 collective-permute-start
  11.9 1.3 collective-permute-start.2
  13.9 2.1 %prepare.1 = (f32[2,3,640,128]{3,2,1,0:T(8,128)S(1)}, f32[2,128,128]{2,1,0:T(8,128)S(1)}, f32[8,128,128]{2,1,0:T(8,128)S(1)}, bf16[768,256]{1,0:T(8,128)(2,1)S(1)}, f32[8,128,128]{2,1,0:T(8,128)}) custom-call(f32[2,512,256]{2,1,0:T(8,128)} %tile.3, f32[2,128,128]{2,1,0:T(8,128)} %probe_in.1, f32[8,128,128]{2,1,0:T(8,128)} %bitcast.16, ...), custom_call_target="tpu_custom_call" | custom-call | tf_op jit(solution)/shard_map/prepare/pallas_call | solution.py:327
  16.0 3.2 %collective-permute-done.2.corner = f32[2,128,128]{2,1,0:T(8,128)S(1)} collective-permute-done((f32[2,128,128]{2,1,0:T(8,128)S(1)}, f32[2,128,128]{2,1,0:T(8,128)S(1)}, u32[]{:S(2)}, u32[]{:S(2)}) %collective-permute-start.2) | collective-permute-done | bytes 131104 | tf_op jit(solution)/shard_map/ppermute | solution.py:33
  19.2 2.7 %collective-permute-done.below = f32[2,128,256]{2,1,0:T(8,128)S(1)} collective-permute-done((f32[2,128,256]{2,1,0:T(8,128)S(1)}, f32[2,128,256]{2,1,0:T(8,128)S(1)}, u32[]{:S(2)}, u32[]{:S(2)}) %collective-permute-start) | collective-permute-done | bytes 262176 | tf_op jit(solution)/shard_map/ppermute | solution.py:20
  21.9 3.0 %first_pass.1 = (f32[2,3,640,128]{3,2,1,0:T(8,128)S(1)}, f32[2,640,128]{2,1,0:T(8,128)S(1)}, f32[2,640,128]{2,1,0:T(8,128)S(1)}, f32[2,640,128]{2,1,0:T(8,128)S(1)}, f32[2,128,128]{2,1,0:T(8,128)S(1)}) custom-call(s32[2,8]{1,0:T(2,128)S(1)} %bitcast.14, s32[1]{0:T(128)} %bitcast.9.counts, f32[2,3,640,128]{3,2,1,0:T(8,128)S(1)} %get-tuple-element.24.ext_in, ...), custom_call_target="tpu_custom_call" | custom-call | tf_op jit(solution)/shard_map/first_pass/pallas_call | solution.py:327
  25.0 6.0 %collective-permute-start.4 = (f32[2,640,128]{2,1,0:T(8,128)S(1)}, f32[2,640,128]{2,1,0:T(8,128)S(1)}, u32[]{:S(2)}, u32[]{:S(2)}) collective-permute-start(f32[2,640,128]{2,1,0:T(8,128)S(1)} %get-tuple-element.32.acc_0), channel_id=1, source_target_pairs={{16,0},{32,16},{48,32},{64,48},{80,64},{96,80},{112,96},{128,112},... | collective-permute-start | bytes 1966088 | tf_op jit(solution)/shard_map/ppermute | solution.py:24
  31.0 1.9 %collective-permute-start.3 = (f32[2,640,128]{2,1,0:T(8,128)S(1)}, f32[2,640,128]{2,1,0:T(8,128)S(1)}, u32[]{:S(2)}, u32[]{:S(2)}) collective-permute-start(f32[2,640,128]{2,1,0:T(8,128)S(1)} %get-tuple-element.34.acc_2), channel_id=1, source_target_pairs={{0,16},{16,32},{32,48},{48,64},{64,80},{80,96},{96,112},{112,128},... | collective-permute-start | bytes 1966088 | tf_op jit(solution)/shard_map/ppermute | solution.py:24
  32.9 12.8 %all_to_all.30.parts = f32[32,8,128]{2,1,0:T(8,128)S(1)} all-to-all(f32[32,8,128]{2,1,0:T(8,128)S(1)} %bitcast.13), channel_id=1, replica_groups={{0,1,2,3,4,5,6,7,8,9,10,11,12,13,14,15,16,17,18,19,20,21,22,23,24,25,26..., dimensions={0} | all-to-all | bytes 262144 | tf_op jit(solution)/shard_map/all_to_all | solution.py:37
  45.8 2.0 %collective-permute-start.5 = (f32[2,3,128,128]{3,2,1,0:T(8,128)S(1)}, f32[2,3,128,128]{3,2,1,0:T(8,128)S(1)}, u32[]{:S(2)}, u32[]{:S(2)}) collective-permute-start(f32[2,3,128,128]{3,2,1,0:T(8,128)S(1)} %get-tuple-element.36), channel_id=1, source_target_pairs={{0,1},{1,2},{2,3},{3,4},{4,5},{5,6},{6,7},{7,8},{8,9},{9,10},{10,1... | collective-permute-start | bytes 1179656 | tf_op jit(solution)/shard_map/ppermute | solution.py:20
  47.9 1.3 collective-permute-start.6
  49.2 25.0 %all_to_all.31.parts = f32[16,8,128]{2,1,0:T(8,128)S(1)} all-to-all(f32[16,8,128]{2,1,0:T(8,128)S(1)} %fold_plane.2.after), channel_id=1, replica_groups={{0,32,64,96,128,160,192,224,256,288,320,352,384,416,448,480},{16,48,80,..., dimensions={0} | all-to-all | bytes 131072 | tf_op jit(solution)/shard_map/all_to_all | solution.py:37
  74.2 17.0 %all_to_all.32 = f32[32,8,128]{2,1,0:T(8,128)S(1)} all-to-all(f32[32,8,128]{2,1,0:T(8,128)S(1)} %fold_line.2), channel_id=1, replica_groups={{0,1,2,3,4,5,6,7,8,9,10,11,12,13,14,15,16,17,18,19,20,21,22,23,24,25,26..., dimensions={0} | all-to-all | bytes 262144 | tf_op jit(solution)/shard_map/all_to_all | solution.py:37
  91.2 5.4 %second_pass.1 = (f32[2,512,256]{2,1,0:T(8,128)}, f32[2,512,128]{2,1,0:T(8,128)}, f32[2,128,128]{2,1,0:T(8,128)}, f32[2,128,128]{2,1,0:T(8,128)}, f32[2,512,128]...) custom-call(s32[2,8]{1,0:T(2,128)S(1)} %bitcast.15, s32[1]{0:T(128)} %bitcast.10.counts, ...), custom_call_target="tpu_custom_call" | custom-call | tf_op jit(solution)/shard_map/second_pass/pallas_call | solution.py:327
  96.6 3.0 %collective-permute-start.7 = (f32[2,512,128]{2,1,0:T(8,128)}, f32[2,512,128]{2,1,0:T(8,128)S(1)}, u32[]{:S(2)}, u32[]{:S(2)}) collective-permute-start(f32[2,512,128]{2,1,0:T(8,128)} %get-tuple-element.42), channel_id=1, source_target_pairs={{0,16},{16,32},{32,48},{48,64},{64,80},{80,96},{96,112},{112,128},... | collective-permute-start | bytes 1572872 | tf_op jit(solution)/shard_map/ppermute | solution.py:24
  99.6 12.9 %all_to_all.33.parts = f32[32,8,128]{2,1,0:T(8,128)S(1)} all-to-all(f32[32,8,128]{2,1,0:T(8,128)} %bitcast.17), channel_id=1, replica_groups={{0,1,2,3,4,5,6,7,8,9,10,11,12,13,14,15,16,17,18,19,20,21,22,23,24,25,26..., dimensions={0} | all-to-all | bytes 262144 | tf_op jit(solution)/shard_map/all_to_all | solution.py:37
  113.2 4.0 %all-to-all-start.4 = ((f32[16,8,128]{2,1,0:T(8,128)}), f32[16,8,128]{2,1,0:T(8,128)S(1)}, u32[]{:S(2)}, u32[]{:S(2)}) async-start(f32[16,8,128]{2,1,0:T(8,128)} %fold_plane.3), calls=%async_computation.4 | async-start | bytes 131072 | tf_op jit(solution)/shard_map/all_to_all | solution.py:37
  117.2 2.0 %collective-permute-start.8 = (f32[2,2,128,128]{3,2,1,0:T(8,128)}, f32[2,2,128,128]{3,2,1,0:T(8,128)S(1)}, u32[]{:S(2)}, u32[]{:S(2)}) collective-permute-start(f32[2,2,128,128]{3,2,1,0:T(8,128)} %get-tuple-element.43), channel_id=1, source_target_pairs={{0,1},{1,2},{2,3},{3,4},{4,5},{5,6},{6,7},{7,8},{8,9},{9,10},{10,1... | collective-permute-start | bytes 786440 | tf_op jit(solution)/shard_map/ppermute | solution.py:20
  119.3 4.9 %collective-permute-start.9 = (f32[2,128,128]{2,1,0:T(8,128)}, f32[2,128,128]{2,1,0:T(8,128)S(1)}, u32[]{:S(2)}, u32[]{:S(2)}) collective-permute-start(f32[2,128,128]{2,1,0:T(8,128)} %get-tuple-element.44), channel_id=1, source_target_pairs={{0,17},{16,33},{32,49},{48,65},{64,81},{80,97},{96,113},{112,129},... | collective-permute-start | bytes 393224 | tf_op jit(solution)/shard_map/ppermute | solution.py:33
  124.1 4.8 %all-to-all-done.4.parts = f32[16,8,128]{2,1,0:T(8,128)S(1)} async-done(((f32[16,8,128]{2,1,0:T(8,128)}), f32[16,8,128]{2,1,0:T(8,128)S(1)}, u32[]{:S(2)}, u32[]{:S(2)}) %all-to-all-start.4) | async-done | bytes 65568 | tf_op jit(solution)/shard_map/all_to_all | solution.py:37
  129.7 5.5 %all-to-all-start.5 = ((f32[32,8,128]{2,1,0:T(8,128)}), f32[32,8,128]{2,1,0:T(8,128)S(1)}, u32[]{:S(2)}, u32[]{:S(2)}) async-start(f32[32,8,128]{2,1,0:T(8,128)} %fold_line.3), calls=%async_computation.5 | async-start | bytes 262144 | tf_op jit(solution)/shard_map/all_to_all | solution.py:37
  135.2 7.5 %all-to-all-done.5 = f32[32,8,128]{2,1,0:T(8,128)S(1)} async-done(((f32[32,8,128]{2,1,0:T(8,128)}), f32[32,8,128]{2,1,0:T(8,128)S(1)}, u32[]{:S(2)}, u32[]{:S(2)}) %all-to-all-start.5) | async-done | bytes 131104 | tf_op jit(solution)/shard_map/all_to_all | solution.py:37
  142.8 2.1 %finish.1 = (f32[2,512,256]{2,1,0:T(8,128)}, f32[2,128,128]{2,1,0:T(8,128)}) custom-call(f32[2,512,256]{2,1,0:T(8,128)} %get-tuple-element.39.obj_in, f32[2,512,128]{2,1,0:T(8,128)} %get-tuple-element.40.side_in, f32[2,128,128]{2,1,0:T(8,128)} %get-tuple-element.41.probe_in, ...), custom_call_target="tpu_custom_call", output_to_operand_aliasing={{0}: (0, {})} | custom-call | tf_op jit(solution)/shard_map/finish/pallas_call | solution.py:327
  (16 shorter events, 2.7 us)
Async XLA Ops:
  0.6 21.3 %copy-start = (s32[1,1,8,2]{2,3,1,0:T(2,128)S(1)}, s32[1,1,8,2]{2,3,1,0:T(2,128)}, u32[]{:S(2)}) copy-start(s32[1,1,8,2]{2,3,1,0:T(2,128)} %param.8) | copy-start | bytes 196
  1.8 20.1 %collective-permute-start.1 = (f32[2,512,128]{2,1,0:T(8,128)S(1)}, f32[2,512,128]{2,1,0:T(8,128)S(1)}, u32[]{:S(2)}, u32[]{:S(2)}) collective-permute-start(f32[2,512,128]{2,1,0:T(8,128)S(1)} %get-tuple-element.26), channel_id=1, source_target_pairs={{16,0},{32,16},{48,32},{64,48},{80,64},{96,80},{112,96},{128,112},... | collective-permute-start | bytes 1572872 | tf_op jit(solution)/shard_map/ppermute | solution.py:24
  10.6 11.3 %collective-permute-start = (f32[2,128,256]{2,1,0:T(8,128)S(1)}, f32[2,128,256]{2,1,0:T(8,128)S(1)}, u32[]{:S(2)}, u32[]{:S(2)}) collective-permute-start(f32[2,128,256]{2,1,0:T(8,128)S(1)} %get-tuple-element.25), channel_id=1, source_target_pairs={{1,0},{2,1},{3,2},{4,3},{5,4},{6,5},{7,6},{8,7},{9,8},{10,9},{11,1... | collective-permute-start | bytes 786440 | tf_op jit(solution)/shard_map/ppermute | solution.py:20
  11.9 7.3 %collective-permute-start.2 = (f32[2,128,128]{2,1,0:T(8,128)S(1)}, f32[2,128,128]{2,1,0:T(8,128)S(1)}, u32[]{:S(2)}, u32[]{:S(2)}) collective-permute-start(f32[2,128,128]{2,1,0:T(8,128)S(1)} %get-tuple-element.27), channel_id=1, source_target_pairs={{17,0},{33,16},{49,32},{65,48},{81,64},{97,80},{113,96},{129,112},... | collective-permute-start | bytes 393224 | tf_op jit(solution)/shard_map/ppermute | solution.py:33
  25.0 20.7 %collective-permute-start.4 = (f32[2,640,128]{2,1,0:T(8,128)S(1)}, f32[2,640,128]{2,1,0:T(8,128)S(1)}, u32[]{:S(2)}, u32[]{:S(2)}) collective-permute-start(f32[2,640,128]{2,1,0:T(8,128)S(1)} %get-tuple-element.32.acc_0), channel_id=1, source_target_pairs={{16,0},{32,16},{48,32},{64,48},{80,64},{96,80},{112,96},{128,112},... | collective-permute-start | bytes 1966088 | tf_op jit(solution)/shard_map/ppermute | solution.py:24
  31.0 14.8 %collective-permute-start.3 = (f32[2,640,128]{2,1,0:T(8,128)S(1)}, f32[2,640,128]{2,1,0:T(8,128)S(1)}, u32[]{:S(2)}, u32[]{:S(2)}) collective-permute-start(f32[2,640,128]{2,1,0:T(8,128)S(1)} %get-tuple-element.34.acc_2), channel_id=1, source_target_pairs={{0,16},{16,32},{32,48},{48,64},{64,80},{80,96},{96,112},{112,128},... | collective-permute-start | bytes 1966088 | tf_op jit(solution)/shard_map/ppermute | solution.py:24
  45.8 45.4 %collective-permute-start.5 = (f32[2,3,128,128]{3,2,1,0:T(8,128)S(1)}, f32[2,3,128,128]{3,2,1,0:T(8,128)S(1)}, u32[]{:S(2)}, u32[]{:S(2)}) collective-permute-start(f32[2,3,128,128]{3,2,1,0:T(8,128)S(1)} %get-tuple-element.36), channel_id=1, source_target_pairs={{0,1},{1,2},{2,3},{3,4},{4,5},{5,6},{6,7},{7,8},{8,9},{9,10},{10,1... | collective-permute-start | bytes 1179656 | tf_op jit(solution)/shard_map/ppermute | solution.py:20
  47.9 43.3 %collective-permute-start.6 = (f32[2,3,128,128]{3,2,1,0:T(8,128)S(1)}, f32[2,3,128,128]{3,2,1,0:T(8,128)S(1)}, u32[]{:S(2)}, u32[]{:S(2)}) collective-permute-start(f32[2,3,128,128]{3,2,1,0:T(8,128)S(1)} %get-tuple-element.37), channel_id=1, source_target_pairs={{1,0},{2,1},{3,2},{4,3},{5,4},{6,5},{7,6},{8,7},{9,8},{10,9},{11,1... | collective-permute-start | bytes 1179656 | tf_op jit(solution)/shard_map/ppermute | solution.py:20
  96.6 46.1 %collective-permute-start.7 = (f32[2,512,128]{2,1,0:T(8,128)}, f32[2,512,128]{2,1,0:T(8,128)S(1)}, u32[]{:S(2)}, u32[]{:S(2)}) collective-permute-start(f32[2,512,128]{2,1,0:T(8,128)} %get-tuple-element.42), channel_id=1, source_target_pairs={{0,16},{16,32},{32,48},{48,64},{64,80},{80,96},{96,112},{112,128},... | collective-permute-start | bytes 1572872 | tf_op jit(solution)/shard_map/ppermute | solution.py:24
  113.2 15.7 %all-to-all-start.4 = ((f32[16,8,128]{2,1,0:T(8,128)}), f32[16,8,128]{2,1,0:T(8,128)S(1)}, u32[]{:S(2)}, u32[]{:S(2)}) async-start(f32[16,8,128]{2,1,0:T(8,128)} %fold_plane.3), calls=%async_computation.4 | async-start | bytes 131072 | tf_op jit(solution)/shard_map/all_to_all | solution.py:37
  117.2 18.0 %collective-permute-start.8 = (f32[2,2,128,128]{3,2,1,0:T(8,128)}, f32[2,2,128,128]{3,2,1,0:T(8,128)S(1)}, u32[]{:S(2)}, u32[]{:S(2)}) collective-permute-start(f32[2,2,128,128]{3,2,1,0:T(8,128)} %get-tuple-element.43), channel_id=1, source_target_pairs={{0,1},{1,2},{2,3},{3,4},{4,5},{5,6},{6,7},{7,8},{8,9},{9,10},{10,1... | collective-permute-start | bytes 786440 | tf_op jit(solution)/shard_map/ppermute | solution.py:20
  119.3 16.0 %collective-permute-start.9 = (f32[2,128,128]{2,1,0:T(8,128)}, f32[2,128,128]{2,1,0:T(8,128)S(1)}, u32[]{:S(2)}, u32[]{:S(2)}) collective-permute-start(f32[2,128,128]{2,1,0:T(8,128)} %get-tuple-element.44), channel_id=1, source_target_pairs={{0,17},{16,33},{32,49},{48,65},{64,81},{80,97},{96,113},{112,129},... | collective-permute-start | bytes 393224 | tf_op jit(solution)/shard_map/ppermute | solution.py:33
  129.7 13.1 %all-to-all-start.5 = ((f32[32,8,128]{2,1,0:T(8,128)}), f32[32,8,128]{2,1,0:T(8,128)S(1)}, u32[]{:S(2)}, u32[]{:S(2)}) async-start(f32[32,8,128]{2,1,0:T(8,128)} %fold_line.3), calls=%async_computation.5 | async-start | bytes 262144 | tf_op jit(solution)/shard_map/all_to_all | solution.py:37
